TPU v7x, 256 devices: a whole 4x4x8 slice. The times are simulated.
256 devices in a mesh: rep: 8 (over z_lo, core), fsdp: 32 (over y, z_hi, x).
Axes of the slice: x: 4, y: 4, z: 8 (z_hi: 2, z_lo: 4; z = z_hi * 4 + z_lo), core: 2. Of those that a mesh axis runs over, the one named last changes fastest.
Arguments:
- activations: bfloat16 [131072, 4096], P(('rep', 'fsdp')), may hold values from -6 to 6
- weights: bfloat16 [8, 4096, 1024], P('rep', 'fsdp'), may hold values from -0.09375 to 0.09375
- cotangent: bfloat16 [131072, 1024], P(('rep', 'fsdp')), may hold values from -6 to 6
- quant_codes: bfloat16 [8, 512, 8192], P('rep', 'fsdp'), may hold values from -6 to 6
- replica_scale: float32 [8], P('rep'), may hold values from 0.25 to 4
- outer_params: float32 [512, 8192], P('fsdp'), may hold values from -6 to 6
- momentum: float32 [512, 8192], P('fsdp'), may hold values from -4 to 4
Outputs:
- projected: bfloat16 [131072, 1024], P(('rep', 'fsdp'))
- input_grad: bfloat16 [131072, 4096], P(('rep', 'fsdp'))
- weight_grad: float32 [8, 4096, 1024], P('rep', 'fsdp')
- new_params: float32 [512, 8192], P('fsdp')
- new_momentum: float32 [512, 8192], P('fsdp')
All inputs are finite; a program needn't handle non-finite values.
Results may differ from a plain program's by a relative error of at most 0.001.
Values may be sent and summed in bfloat16 or wider, within the bound.
No kernel may reach another device: no remote copies, remote signals or barrier semaphores. Data moves between devices by JAX's collectives and lax.ppermute only.
A program may use at most 128 MiB of HBM per device.

v0:
```python
import jax
import jax.numpy as jnp
from jax import lax
from jax.sharding import PartitionSpec as P


def outer_step(average, params_rows, moment_rows):
    moment_next = 0.9 * moment_rows + average
    params_next = params_rows - 0.7 * (average + 0.9 * moment_next)
    return (params_next, moment_next)


def local(activations, weights, cotangent, quant_codes, replica_scale, outer_params, momentum):
    shard = weights[0]
    tokens_here = activations.shape[0]
    columns = activations
    forward = jnp.dot(
        columns,
        lax.all_gather(shard, "fsdp", axis=0, tiled=True),
        preferred_element_type=jnp.float32,
    )
    backward = jnp.einsum(
        "tk,dk->td",
        cotangent,
        lax.all_gather(shard, "fsdp", axis=0, tiled=True),
        preferred_element_type=jnp.float32,
    )
    replica_tokens = tokens_here * lax.axis_size("fsdp")
    factor = 1.0 / jnp.sqrt(jnp.float32(replica_tokens))
    columns = activations
    gradient = lax.psum_scatter(
        jnp.einsum("td,tk->dk", columns, cotangent, preferred_element_type=jnp.float32) * factor,
        "fsdp",
        scatter_dimension=0,
        tiled=True,
    )
    replicas = lax.axis_size("rep")
    dequant = replica_scale[0] * quant_codes[0].astype(jnp.float32)
    summed = lax.psum(dequant, "rep")
    new_params, new_momentum = outer_step(summed / replicas, outer_params, momentum)
    return (
        forward.astype(jnp.bfloat16),
        backward.astype(jnp.bfloat16),
        gradient[None],
        new_params,
        new_momentum,
    )


def solution(mesh):
    placed = (
        P(("rep", "fsdp"), None),
        P("rep", "fsdp", None),
        P(("rep", "fsdp"), None),
        P("rep", "fsdp", None),
        P("rep"),
        P("fsdp", None),
        P("fsdp", None),
    )
    return jax.shard_map(
        local,
        mesh=mesh,
        in_specs=placed,
        out_specs=(
            P(("rep", "fsdp"), None),
            P(("rep", "fsdp"), None),
            P("rep", "fsdp", None),
            P("fsdp", None),
            P("fsdp", None),
        ),
        check_vma=False,
    )
```

profile of v0, /device:TPU:24, one launch (start us, length us, event | category | flops | bytes accessed | tf_op | source)
XLA Modules:
  0.0 573.0 jit_solution(3807620684508528240)
XLA Ops:
  8.0 0.0 copy-start
  8.0 0.0 all-reduce.2.cloned.1.call-start
  8.8 1.8 multiply_bitcast_fusion
  10.6 0.0 all-reduce.2.cloned.1.call-update
  10.6 0.0 all-gather.3.cloned.1.call-start
  10.6 0.5 all-gather.3.cloned.1.call-update
  11.2 0.0 reduce-scatter.2.cloned.1.call-start
  11.2 0.0 copy-done
  11.2 10.4 %broadcast_multiply_fusion = f32[4096,1024]{1,0:T(8,128)} fusion(bf16[512,4096]{1,0:T(8,128)(2,1)} %param.7, bf16[512,1024]{1,0:T(8,128)(2,1)S(1)} %copy-done), kind=kOutput, calls=%fused_computation.4 | convolution fusion | flops 4299161600 | bytes 22020096 | tf_op jit(solution)/shard_map/td,tk->dk/dot_general | solution.py:32
  21.6 0.0 copy-start.1
  21.6 0.0 copy-start.2
  21.6 0.0 reduce-scatter.2.cloned.1.call-update
  21.6 72.3 %all-reduce.2.cloned.1.call-done = f32[16,8192]{1,0:T(8,128)} async-done(((f32[16,8192]{1,0:T(8,128)}), f32[16,8192]{1,0:T(8,128)}) %all-reduce.2.cloned.1.call-update) | async-done | bytes 524304 | tf_op jit(solution)/shard_map/psum | solution.py:39
  94.0 0.0 copy-done.1
  94.0 0.0 copy-done.2
  94.0 2.1 multiply_subtract_fusion
  96.1 76.5 %all-gather.3.cloned.1.call-done = bf16[1,4096,1024]{2,1,0:T(8,128)(2,1)} async-done(((bf16[1,128,1024]{2,1,0:T(8,128)(2,1)}), bf16[1,4096,1024]{2,1,0:T(8,128)(2,1)}) %all-gather.3.cloned.1.call-update) | async-done | bytes 8388624 | tf_op jit(solution)/shard_map/all_gather | solution.py:19
  172.6 0.0 copy-start.3
  172.6 0.0 copy-start.4
  172.6 9.6 %fusion.4 = bf16[512,4096]{1,0:T(8,128)(2,1)} fusion(bf16[512,1024]{1,0:T(8,128)(2,1)S(1)} %copy-done, bf16[1,4096,1024]{2,1,0:T(8,128)(2,1)} %all-gather.3.cloned.1.call-done), kind=kOutput, calls=%fused_computation.5 | convolution fusion | flops 4297064448 | bytes 13631488 | tf_op jit(solution)/shard_map/tk,dk->td/dot_general | solution.py:22
  182.2 0.0 copy-done.3
  182.2 0.0 copy-done.4
  182.2 5.5 fusion.7
  187.7 377.8 %reduce-scatter.2.cloned.1.call-done = f32[128,1024]{1,0:T(8,128)} async-done(((f32[4096,1024]{1,0:T(8,128)}), f32[128,1024]{1,0:T(8,128)}) %reduce-scatter.2.cloned.1.call-update) | async-done | bytes 524304 | tf_op jit(solution)/shard_map/reduce_scatter | solution.py:31
Async XLA Ops:
  8.0 3.2 copy-start
  8.0 86.0 %all-reduce.2.cloned.1.call-start = ((), (), s32[]{:S(2)}) async-start(), calls=%async_computation.2 | async-start | bytes 1048576 | tf_op jit(solution)/shard_map/psum | solution.py:39
  10.6 162.0 %all-gather.3.cloned.1.call-start = ((), (), s32[]{:S(2)}) async-start(), calls=%async_computation.3 | async-start | bytes 8650752 | tf_op jit(solution)/shard_map/all_gather | solution.py:19
  11.2 554.4 %reduce-scatter.2.cloned.1.call-start = ((), (), s32[]{:S(2)}) async-start(), calls=%async_computation.1 | async-start | bytes 17301504 | tf_op jit(solution)/shard_map/reduce_scatter | solution.py:31
  21.6 72.4 %copy-start.1 = (f32[16,8192]{1,0:T(8,128)S(1)}, f32[16,8192]{1,0:T(8,128)}, u32[]{:S(2)}) copy-start(f32[16,8192]{1,0:T(8,128)} %param.12) | copy-start | bytes 1572868
  21.6 72.4 %copy-start.2 = (f32[16,8192]{1,0:T(8,128)S(1)}, f32[16,8192]{1,0:T(8,128)}, u32[]{:S(2)}) copy-start(f32[16,8192]{1,0:T(8,128)} %param.13) | copy-start | bytes 1572868
  172.6 9.6 %copy-start.3 = (bf16[1,4096,1024]{2,1,0:T(8,128)(2,1)S(1)}, bf16[1,4096,1024]{2,1,0:T(8,128)(2,1)}, u32[]{:S(2)}) copy-start(bf16[1,4096,1024]{2,1,0:T(8,128)(2,1)} %all-gather.3.cloned.1.call-done) | copy-start | bytes 25165828
  172.6 9.6 %copy-start.4 = (bf16[512,4096]{1,0:T(8,128)(2,1)S(1)}, bf16[512,4096]{1,0:T(8,128)(2,1)}, u32[]{:S(2)}) copy-start(bf16[512,4096]{1,0:T(8,128)(2,1)} %param.7) | copy-start | bytes 12582916
Sparse Core Ops, SparseCore 0:
  12.1 81.8 all-reduce.1
Sparse Core Ops, SparseCore 1:
  14.6 157.9 all-gather.2
  175.6 389.9 reduce-scatter.1
where the time goes:
time: 581 us; the launch traced here: 573 us
  waiting for transfers between devices  527 us (91%)
  matrix products  25.5 us (4%)
  between operations  16.2 us (3%)
    reduce_scatter x1, waiting for transfers between devices, local(): lax.psum_scatter(jnp.einsum('td,tk->dk', columns, cotangent, preferred_el...  378 us
    all_gather x1, waiting for transfers between devices, local(): lax.all_gather(shard, 'fsdp', axis=0, tiled=True)  76.5 us
    psum x1, waiting for transfers between devices, local(): summed = lax.psum(dequant, 'rep')  72.3 us
  transfers between devices with their start and end apart: 3, of which 3 were waited for; matrix products, arithmetic and copies ran while one was open for 5% of the time, Pallas kernels for 0%

commit v1 on v0

v1 whole, which is shorter than its diff:
```python
import jax
import jax.numpy as jnp
from jax import lax
from jax.experimental import pallas as pl
from jax.experimental.pallas import tpu as pltpu
from jax.sharding import PartitionSpec as P

NX, NY, NZ, NR = 4, 4, 2, 8
NOTE = 16
LOW = 512
F32, F16, BF16 = jnp.float32, jnp.float16, jnp.bfloat16


def place():
    i = lax.axis_index("fsdp")
    x, y, z = i % NX, i // (NX * NZ), (i // NX) % NZ
    turned = lax.axis_index("rep") % 2
    return x + turned * (y - x), y + turned * (x - y), z, turned


def feature_block(u, v, z, turned):
    x, y = u + turned * (v - u), v + turned * (u - v)
    return (y * NZ + z) * NX + x


def move(a, change):
    pairs = []
    for r in range(NR):
        for y in range(NY):
            for z in range(NZ):
                for x in range(NX):
                    u, v, w = change(*((y, x) if r % 2 else (x, y)), z)
                    to_x, to_y = (v, u) if r % 2 else (u, v)
                    here = (y * NZ + z) * NX + x
                    there = ((to_y % NY) * NZ + w % NZ) * NX + to_x % NX
                    pairs.append((r * NX * NY * NZ + here, r * NX * NY * NZ + there))
    return lax.ppermute(a, ("rep", "fsdp"), pairs)


STEPS = {
    "u+": lambda u, v, z: (u + 1, v, z),
    "u-": lambda u, v, z: (u - 1, v, z),
    "v+": lambda u, v, z: (u, v + 1, z),
    "v-": lambda u, v, z: (u, v - 1, z),
    "z": lambda u, v, z: (u, v, z + 1),
    "uu": lambda u, v, z: (u + 2, v, z),
    "vv": lambda u, v, z: (u, v + 2, z),
}


def after(a, *others):
    return lax.optimization_barrier((a, others))[0]


BUFFERS = (
    ((2, 0), (2, 1), (3, 2), (3, 3)),
    ((2, 2), (2, 3), (1, 0), (1, 1)),
    ((3, 0), (3, 1), (1, 2), (1, 3)),
    ((0, 0), (0, 1), (0, 2), (0, 3)),
)


CHUNK = 64


def sort_kernel(act, cot, out, top, act_s, cot_s, out_s, in_sem, out_sem):
    u, v, z, turned = place()
    count = act.shape[0] // CHUNK
    for c in range(count):
        rows = pl.ds(c * CHUNK, CHUNK)
        pltpu.make_async_copy(act.at[rows], act_s.at[c], in_sem.at[0, c]).start()
        pltpu.make_async_copy(cot.at[rows], cot_s.at[c], in_sem.at[1, c]).start()

    def fold(value):
        m = None
        for i in range(value.shape[1] // 128):
            part = jnp.abs(value[:, i * 128 : (i + 1) * 128])
            m = part if m is None else jnp.maximum(m, part)
        return jnp.max(m.astype(F32).reshape(-1, 8, 128), axis=0)

    top[...] = jnp.zeros_like(top)

    @pl.loop(0, count)
    def _(c):
        pltpu.make_async_copy(act_s.at[c], act_s.at[c], in_sem.at[0, c]).wait()
        pltpu.make_async_copy(cot_s.at[c], cot_s.at[c], in_sem.at[1, c]).wait()
        for p in range(NZ):
            for b, slots in enumerate(BUFFERS):
                for k, (ju, jv) in enumerate(slots):
                    block = feature_block((u - ju) & 3, (v - jv) & 3, z ^ p, turned)
                    lanes = pl.ds(pl.multiple_of(block * 128, 128), 128)
                    out_s[c, p, b, :, k * 128 : (k + 1) * 128] = act_s[c, :, lanes]
        top[0] = jnp.maximum(top[0], fold(act_s[c]))
        top[1] = jnp.maximum(top[1], fold(cot_s[c]))
        rows = pl.ds(pl.multiple_of(c * CHUNK, CHUNK), CHUNK)
        pltpu.make_async_copy(out_s.at[c], out.at[:, :, rows], out_sem.at[c]).start()

    for c in range(count):
        pltpu.make_async_copy(out_s.at[c], out_s.at[c], out_sem.at[c]).wait()


def sort(act, cot):
    count = act.shape[0] // CHUNK
    any_ = pl.BlockSpec(memory_space=pl.ANY)
    return pl.pallas_call(
        sort_kernel,
        in_specs=[any_, any_],
        out_specs=[any_, pl.BlockSpec(memory_space=pltpu.VMEM)],
        out_shape=[
            jax.ShapeDtypeStruct((NZ, NX, act.shape[0], 512), BF16),
            jax.ShapeDtypeStruct((2, 8, 128), F32),
        ],
        scratch_shapes=[
            pltpu.VMEM((count, CHUNK, act.shape[1]), BF16),
            pltpu.VMEM((count, CHUNK, cot.shape[1]), BF16),
            pltpu.VMEM((count, NZ, NX, CHUNK, 512), BF16),
            pltpu.SemaphoreType.DMA((2, count)),
            pltpu.SemaphoreType.DMA((count,)),
        ],
        compiler_params=pltpu.CompilerParams(vmem_limit_bytes=56 << 20),
        cost_estimate=pl.CostEstimate(flops=0, bytes_accessed=1 << 20, transcendentals=0),
    )(act, cot)


def product_kernel(counts, before, *refs):
    act, cot = refs[0], refs[1]
    n = 2 + sum(counts.values())
    pieces = list(refs[2:n])
    partial = refs[n] if before else None
    n += 2 if before else 0
    proj, grad = refs[n], refs[n + 1]
    act_s, cot_s, w_s, acc_s, grad_s, a_sem, w_sem, c_sem, o_sem, p_sem = refs[n + 2 :]
    u, v, z, turned = place()

    def columns(p, ju, jv):
        block = feature_block((u - ju) & 3, (v - jv) & 3, z ^ p, turned)
        return pl.ds(pl.multiple_of(block * 128, 128), 128)

    cot_in = pltpu.make_async_copy(cot, cot_s, c_sem)
    cot_in.start()
    if before:
        sums_in = pltpu.make_async_copy(partial, acc_s, p_sem)
        sums_in.start()
    units = []
    for j, count in counts.items():
        halves = []
        for _ in range(count):
            part = pieces.pop(0)
            halves += [(part, begin) for begin in (0, LOW) if begin < part.shape[0]]
        units += [(p, j, [(part, begin + p * 256) for part, begin in halves]) for p in range(NZ)]
    for k, (p, j, halves) in enumerate(units):
        for h, (part, begin) in enumerate(halves):
            to = w_s.at[k, pl.ds(h * 256, 256)]
            pltpu.make_async_copy(part.at[pl.ds(begin, 256)], to, w_sem.at[k]).start()
        for i in range(NX):
            to = act_s.at[k, :, pl.ds(i * 128, 128)]
            pltpu.make_async_copy(act.at[:, columns(p, i, j)], to, a_sem.at[k]).start()
    cot_in.wait()
    if before:
        sums_in.wait()
    for k, (p, j, _) in enumerate(units):
        pltpu.make_async_copy(w_s.at[k], w_s.at[k], w_sem.at[k]).wait()
        pltpu.make_async_copy(act_s.at[k], act_s.at[k], a_sem.at[k]).wait()
        w = w_s[k]
        term = jnp.dot(act_s[k], w, preferred_element_type=F32)
        if k == 0 and not before:
            acc_s[...] = term
        else:
            acc_s[...] += term
        grad_s[k] = lax.dot_general(
            cot_s[...], w, (((1,), (1,)), ((), ())), preferred_element_type=F32
        ).astype(BF16)
        for i in range(NX):
            out = grad_s.at[k, :, pl.ds(i * 128, 128)]
            pltpu.make_async_copy(out, grad.at[:, columns(p, i, j)], o_sem.at[k]).start()
    proj[...] = acc_s[...].astype(proj.dtype)
    for k in range(len(units)):
        pltpu.make_async_copy(grad_s.at[k], grad_s.at[k], o_sem.at[k]).wait()


def products(act, cot, pieces, before=(), last=False):
    tokens, depth = act.shape
    width = cot.shape[1]
    counts = {j: len(parts) for j, parts in pieces.items()}
    flat = [part for parts in pieces.values() for part in parts]
    n = NZ * len(pieces)
    any_ = pl.BlockSpec(memory_space=pl.ANY)
    args = [act, cot, *flat, *before]
    return pl.pallas_call(
        lambda *refs: product_kernel(counts, bool(before), *refs),
        in_specs=[any_] * len(args),
        out_specs=[pl.BlockSpec(memory_space=pltpu.VMEM), any_],
        out_shape=[
            jax.ShapeDtypeStruct((tokens, width), BF16 if last else F32),
            jax.ShapeDtypeStruct((tokens, depth), BF16),
        ],
        input_output_aliases={len(args) - 1: 1} if before else {},
        scratch_shapes=[
            pltpu.VMEM((n, tokens, 512), BF16),
            pltpu.VMEM((tokens, width), BF16),
            pltpu.VMEM((n, 512, width), BF16),
            pltpu.VMEM((tokens, width), F32),
            pltpu.VMEM((n, tokens, 512), BF16),
            pltpu.SemaphoreType.DMA((n,)),
            pltpu.SemaphoreType.DMA((n,)),
            pltpu.SemaphoreType.DMA,
            pltpu.SemaphoreType.DMA((n,)),
            pltpu.SemaphoreType.DMA,
        ],
        compiler_params=pltpu.CompilerParams(vmem_limit_bytes=(8 + 3 * n) << 20),
        cost_estimate=pl.CostEstimate(flops=0, bytes_accessed=1 << 20, transcendentals=0),
    )(*args)


class Lanes:
    def __init__(self):
        self.last = {}

    def queue(self, lane, a, shift):
        if lane in self.last:
            a = after(a, self.last[lane])
        r = shift(a)
        self.last[lane] = r
        return r

    def send(self, lane, a, step=None):
        return self.queue(lane, a, lambda a: move(a, STEPS[step or lane]))

    def both(self, axis, forward, backward, lane=""):
        up, down = axis + "+", axis + "-"
        pair = self.send(lane + up, forward, up), self.send(lane + down, backward, down)
        return lax.optimization_barrier(pair)


def gather_v(lanes, a):
    f, b = lanes.both("v", a, a)
    low, high = lanes.both("v", f[:LOW], b[LOW:])
    return [a, f, low, high, b]


def join_kernel(cuts, *refs):
    arrays, out, sem = refs[:-2], refs[-2], refs[-1]
    copies = []
    for k, (which, begin, rows) in enumerate(cuts):
        from_ = arrays[which].at[pl.ds(begin, rows)]
        copies.append(pltpu.make_async_copy(from_, out.at[pl.ds(k * rows, rows)], sem.at[k]))
    for copy in copies:
        copy.start()
    for copy in copies:
        copy.wait()


def join(arrays, cuts):
    width = arrays[0].shape[1]
    total = sum(rows for _, _, rows in cuts)
    any_ = pl.BlockSpec(memory_space=pl.ANY)
    return pl.pallas_call(
        lambda *refs: join_kernel(cuts, *refs),
        in_specs=[any_] * len(arrays),
        out_specs=any_,
        out_shape=jax.ShapeDtypeStruct((total, width), arrays[0].dtype),
        scratch_shapes=[pltpu.SemaphoreType.DMA((len(cuts),))],
        compiler_params=pltpu.CompilerParams(vmem_limit_bytes=1 << 20),
        cost_estimate=pl.CostEstimate(flops=0, bytes_accessed=1 << 20, transcendentals=0),
    )(*arrays)


def gather_u(lanes, near, far, note):
    n = near.shape[0]
    own = jnp.concatenate([near, far, note], axis=0)
    f, o, b = all_of_ring(lanes, "u", own, own, own)
    row = join((own, f, o, b), [(m, p * n, n) for pair in ((0, 1), (2, 3)) for p in range(NZ) for m in pair])
    notes = [x[2 * n :, :128].astype(F32) for x in (own, f, o, b)]
    return row, jnp.maximum(jnp.maximum(notes[0], notes[1]), jnp.maximum(notes[2], notes[3]))


def all_of_ring(lanes, axis, up, far, down, lane=""):
    f, b = lanes.both(axis, up, down, lane)
    return f, lanes.send(lane + "e", far, 2 * axis), b


def wide(*parts):
    total = parts[0].astype(F32)
    for p in parts[1:]:
        total = total + p.astype(F32)
    return total


def first_sums(buffers, arrived):
    half = buffers[0].shape[0] // 2
    f, b = arrived
    up = wide(buffers[2][:half], f[:half]).astype(F16)
    down = wide(buffers[2][half:], b[:half]).astype(F16)
    return up, down


def last_sums(buffers, arrived, sums):
    half = buffers[0].shape[0] // 2
    f, b = arrived
    f2, b2 = sums
    low = wide(buffers[3][:half], b[half:], f2)
    high = wide(buffers[3][half:], f[half:], b2)
    return [part.astype(F16) for part in (low, high)]


def with_note(a, exponent):
    note = jnp.broadcast_to(exponent.astype(F16), (NOTE, a.shape[1]))
    return jnp.concatenate([a, note], axis=0)


def exponent_in(a):
    return a[-NOTE : 1 - NOTE].astype(F32)


def reduce_v(lanes, low, high, exponent, behind, lane=""):
    n = low.shape[0] // 2
    low, high = after((low, high), *behind)
    sent = [with_note(part, exponent) for part in (high[n:], high[:n], low[n:])]
    got = all_of_ring(lanes, "v", *sent, lane)
    exponents = [exponent_in(part) for part in got]
    least = exponent
    for e in exponents:
        least = jnp.minimum(least, e)
    total = low[:n].astype(F32) * jnp.exp2(least - exponent)
    for part, e in zip(got, exponents):
        total = total + part[:-NOTE].astype(F32) * jnp.exp2(least - e)
    return total, least


def terms(act_sorted, cot, scale):
    out = []
    for part in act_sorted:
        g = jnp.einsum("td,tk->dk", part, cot, preferred_element_type=F32)
        out.append((g * scale).astype(F16))
    return out


def sum_of_replicas(lanes, codes, scale, phases):
    total = codes.astype(F32) * scale
    for bit in (1, 2, 4):
        pairs = [(j, j ^ bit) for j in range(NR)]
        if bit > 1:
            total = after(total, phases[bit // 2 - 1])
        total = total + lanes.queue("r", total, lambda a: lax.ppermute(a, "rep", pairs))
    return total


def exponent_for(note, tokens):
    bound = note[0, 0] * note[NOTE // 2, 0] * tokens
    return jnp.floor(jnp.log2(32768.0 / jnp.maximum(bound, 1e-30)))


def outer_step(average, params_rows, moment_rows):
    moment_next = 0.9 * moment_rows + average
    params_next = params_rows - 0.7 * (average + 0.9 * moment_next)
    return params_next, moment_next


def local(activations, weights, cotangent, quant_codes, replica_scale, outer_params, momentum):
    tokens = activations.shape[0] * lax.axis_size("fsdp")
    lanes = Lanes()
    shard = weights[0]
    far_shard = lanes.send("z", shard)
    act_sorted, top = sort(activations, cotangent)
    note = jnp.broadcast_to(jnp.max(top, axis=(1, 2))[:, None, None], (2, NOTE // 2, shard.shape[1]))
    row, note = gather_u(lanes, shard, far_shard, note.reshape(NOTE, -1).astype(BF16))
    exponent = exponent_for(note, tokens)
    scale = after(jnp.exp2(exponent), row)
    theirs = terms(act_sorted[1][:2], cotangent, scale)
    own, below, far_low, far_high, above = gather_v(lanes, row)
    theirs_in = lanes.both("u", theirs[0], theirs[1])
    phases = (far_shard, row)
    average = sum_of_replicas(lanes, quant_codes[0], replica_scale[0], phases) / lax.axis_size("rep")
    ready = after(cotangent, theirs, average)
    part = products(activations, ready, {0: [own]})
    theirs += terms(act_sorted[1][2:], ready, scale)
    mine = terms(act_sorted[0], cotangent, after(scale, theirs_in))

    sums = after(first_sums(theirs, theirs_in), below, above, part)
    theirs = last_sums(theirs, theirs_in, lanes.both("u", *sums))
    mine_in = lanes.both("u", *after((mine[0], mine[1]), far_low, far_high))
    theirs, their_exponent = reduce_v(lanes, *theirs, exponent, (), "theirs ")
    theirs = with_note(theirs.astype(F16), their_exponent)
    part = products(activations, after(cotangent, theirs), {1: [below], 3: [above]}, part)

    sums = after(first_sums(mine, mine_in), theirs, part)
    theirs = lanes.send("z", theirs)
    projected, input_grad = products(activations, after(cotangent, sums), {2: [far_low, far_high]}, part, last=True)
    mine = last_sums(mine, mine_in, lanes.both("u", *sums))
    mine, my_exponent = reduce_v(lanes, *mine, exponent, (projected, input_grad))
    total = mine * jnp.exp2(-my_exponent) + theirs[:-NOTE].astype(F32) * jnp.exp2(-exponent_in(theirs))
    gradient = total * (1.0 / jnp.sqrt(jnp.float32(tokens)))

    new_params, new_momentum = outer_step(average, outer_params, momentum)
    return projected, input_grad, gradient[None], new_params, new_momentum


def solution(mesh):
    placed = (
        P(("rep", "fsdp"), None),
        P("rep", "fsdp", None),
        P(("rep", "fsdp"), None),
        P("rep", "fsdp", None),
        P("rep"),
        P("fsdp", None),
        P("fsdp", None),
    )
    return jax.shard_map(
        local,
        mesh=mesh,
        in_specs=placed,
        out_specs=(
            P(("rep", "fsdp"), None),
            P(("rep", "fsdp"), None),
            P("rep", "fsdp", None),
            P("fsdp", None),
            P("fsdp", None),
        ),
        check_vma=False,
    )
```

time: 581 us -> 156 us (0.27); the launches traced: 573 us -> 155 us
  waiting for transfers between devices: 527 us -> 43.2 us
  starting transfers between devices: 0.12 us -> 66.5 us
  Pallas kernels: 0 us -> 21.5 us
  matrix products: 25.5 us -> 7.11 us
  between operations: 16.2 us -> 3.11 us
  other arithmetic: 3.92 us -> 9.8 us
    reduce_scatter x1 -> x0, waiting for transfers between devices: 378 us -> none  [local(): lax.psum_scatter(jnp.einsum('td,tk->dk', columns, cotangent, preferred_el...]
    all_gather x1 -> x0, waiting for transfers between devices: 76.5 us -> none  [local(): lax.all_gather(shard, 'fsdp', axis=0, tiled=True)]
    psum x1 -> x0, waiting for transfers between devices: 72.3 us -> none  [local(): summed = lax.psum(dequant, 'rep')]
    ppermute x0 -> x26, starting transfers between devices: none -> 66.5 us  [the longest x23 54.4 us: move(): return lax.ppermute(a, ('rep', 'fsdp'), pairs)]
    ppermute x0 -> x26, waiting for transfers between devices: none -> 43.2 us  [the longest x23 28.2 us: move(): return lax.ppermute(a, ('rep', 'fsdp'), pairs)]
    pallas_call x0 -> x5, Pallas kernels: none -> 21.5 us  [the longest x3 16.3 us: products(): pl.pallas_call(lambda *refs: product_kernel(counts, bool(before), *refs),...]
    dot_general x3 -> x8, matrix products: 25.5 us -> 7.11 us  [terms(): g = jnp.einsum('td,tk->dk', part, cot, preferred_element_type=F32)]
  transfers between devices with their start and end apart: 3 -> 26, of which waited for: 3 -> 10; matrix products, arithmetic and copies ran while one was open for 5% -> 12% of each run, Pallas kernels for 0% -> 14%
where the time goes in v1:
time: 156 us; the launch traced here: 155 us
  starting transfers between devices  66.5 us (43%)
  waiting for transfers between devices  43.2 us (28%)
  Pallas kernels  21.5 us (14%)
  other arithmetic  9.8 us (6%)
  matrix products  7.11 us (5%)
  local copies, waits for them, and re-layouts  3.71 us (2%)
  between operations  3.11 us (2%)
    ppermute x23, starting transfers between devices, move(): return lax.ppermute(a, ('rep', 'fsdp'), pairs)  54.4 us
    ppermute x23, waiting for transfers between devices, move(): return lax.ppermute(a, ('rep', 'fsdp'), pairs)  28.2 us
    pallas_call x3, Pallas kernels, products(): pl.pallas_call(lambda *refs: product_kernel(counts, bool(before), *refs),...  16.3 us
    ppermute x3, waiting for transfers between devices, sum_of_replicas(): lax.ppermute(a, 'rep', pairs)  15 us
    ppermute x3, starting transfers between devices, sum_of_replicas(): lax.ppermute(a, 'rep', pairs)  12.1 us
    dot_general x8, matrix products, terms(): g = jnp.einsum('td,tk->dk', part, cot, preferred_element_type=F32)  7.11 us
    pallas_call x1, Pallas kernels, sort(): pl.pallas_call(sort_kernel, in_specs=[any_, any_], out_specs=[any_, pl.Bl...  4.97 us
  transfers between devices with their start and end apart: 26, of which 10 were waited for; matrix products, arithmetic and copies ran while one was open for 12% of the time, Pallas kernels for 14%

profile of v1, /device:TPU:24, one launch (start us, length us, event | category | flops | bytes accessed | tf_op | source)
XLA Modules:
  0.0 154.9 jit_solution(18003054438701402116)
XLA Ops:
  2.4 7.3 %collective-permute-start = (bf16[128,1024]{1,0:T(8,128)(2,1)}, bf16[128,1024]{1,0:T(8,128)(2,1)S(1)}, u32[]{:S(2)}, u32[]{:S(2)}) collective-permute-start(bf16[128,1024]{1,0:T(8,128)(2,1)} %bitcast.53), channel_id=1, source_target_pairs={{0,4},{1,5},{2,6},{3,7},{4,0},{5,1},{6,2},{7,3},{8,12},{9,13},{10,... | collective-permute-start | bytes 786440 | tf_op jit(solution)/shard_map/ppermute | solution.py:37
  9.7 5.0 %shard_map.110 = (bf16[2,4,512,512]{3,2,1,0:T(8,128)(2,1)}, f32[2,8,128]{2,1,0:T(8,128)}) custom-call(bf16[512,4096]{1,0:T(8,128)(2,1)} %refs_0_.5, bf16[512,1024]{1,0:T(8,128)(2,1)} %refs_1_.2), custom_call_target="tpu_custom_call" | custom-call | bytes 1048576 | tf_op jit(solution)/shard_map/pallas_call | solution.py:105
  15.6 2.3 %collective-permute-done = bf16[128,1024]{1,0:T(8,128)(2,1)S(1)} collective-permute-done((bf16[128,1024]{1,0:T(8,128)(2,1)}, bf16[128,1024]{1,0:T(8,128)(2,1)S(1)}, u32[]{:S(2)}, u32[]{:S(2)}) %collective-permute-start) | collective-permute-done | bytes 262176 | tf_op jit(solution)/shard_map/ppermute | solution.py:37
  18.1 3.1 %collective-permute-start.3 = (bf16[272,1024]{1,0:T(8,128)(2,1)S(1)}, bf16[272,1024]{1,0:T(8,128)(2,1)S(1)}, u32[]{:S(2)}, u32[]{:S(2)}) collective-permute-start(bf16[272,1024]{1,0:T(8,128)(2,1)S(1)} %maximum_maximum_fusion.refs_0_), channel_id=1, source_target_pairs={{0,2},{1,3},{2,0},{3,1},{4,6},{5,7},{6,4},{7,5},{8,10},{9,11},{10,... | collective-permute-start | bytes 1671176 | tf_op jit(solution)/shard_map/ppermute | solution.py:37
  21.2 1.1 collective-permute-start.2
  24.1 5.6 %collective-permute-start.11 = (f32[16,8192]{1,0:T(8,128)}, f32[16,8192]{1,0:T(8,128)}, u32[]{:S(2)}, u32[]{:S(2)}) collective-permute-start(f32[16,8192]{1,0:T(8,128)} %fusion.16), channel_id=1, source_target_pairs={{0,64},{32,96},{64,0},{96,32},{128,192},{160,224},{192,128},{224,1... | collective-permute-start | bytes 1572872 | tf_op jit(solution)/shard_map/ppermute | solution.py:344
  29.7 5.6 %collective-permute-done.2.refs_3_ = bf16[272,1024]{1,0:T(8,128)(2,1)S(1)} collective-permute-done((bf16[272,1024]{1,0:T(8,128)(2,1)S(1)}, bf16[272,1024]{1,0:T(8,128)(2,1)S(1)}, u32[]{:S(2)}, u32[]{:S(2)}) %collective-permute-start.2) | collective-permute-done | bytes 557088 | tf_op jit(solution)/shard_map/ppermute | solution.py:37
  36.4 2.5 %collective-permute-start.6 = (bf16[1024,1024]{1,0:T(8,128)(2,1)S(1)}, bf16[1024,1024]{1,0:T(8,128)(2,1)}, u32[]{:S(2)}, u32[]{:S(2)}) collective-permute-start(bf16[1024,1024]{1,0:T(8,128)(2,1)S(1)} %shard_map.111.refs_2_), channel_id=1, source_target_pairs={{0,8},{1,9},{2,10},{3,11},{4,12},{5,13},{6,14},{7,15},{8,16},{9,17... | collective-permute-start | bytes 6291464 | tf_op jit(solution)/shard_map/ppermute | solution.py:37
  40.9 1.4 add.81
  42.3 6.4 %collective-permute-start.12 = (f32[16,8192]{1,0:T(8,128)S(1)}, f32[16,8192]{1,0:T(8,128)S(1)}, u32[]{:S(2)}, u32[]{:S(2)}) collective-permute-start(f32[16,8192]{1,0:T(8,128)S(1)} %add.81), channel_id=1, source_target_pairs={{0,128},{32,160},{64,192},{96,224},{128,0},{160,32},{192,64},{224,... | collective-permute-start | bytes 1572872 | tf_op jit(solution)/shard_map/ppermute | solution.py:344
  48.8 1.9 %multiply_convert_fusion.6 = f16[512,1024]{1,0:T(8,128)(2,1)S(1)} fusion(bf16[512,1024]{1,0:T(8,128)(2,1)S(1)} %copy-done.1, f32[]{:T(128)S(6)} %exp2.67, bf16[2,4,512,512]{3,2,1,0:T(8,128)(2,1)} %get-tuple-element.64), kind=kOutput, calls=%fused_computation.6 | convolution fusion | flops 537919488 | bytes 2621444 | tf_op jit(solution)/shard_map/td,tk->dk/dot_general | solution.py:333
  51.4 1.5 collective-permute-start.4
  52.9 1.8 %collective-permute-start.5 = (f16[512,1024]{1,0:T(8,128)(2,1)S(1)}, f16[512,1024]{1,0:T(8,128)(2,1)S(1)}, u32[]{:S(2)}, u32[]{:S(2)}) collective-permute-start(f16[512,1024]{1,0:T(8,128)(2,1)S(1)} %multiply_convert_fusion.6), channel_id=1, source_target_pairs={{0,3},{1,0},{2,1},{3,2},{4,7},{5,4},{6,5},{7,6},{8,11},{9,8},{10,9... | collective-permute-start | bytes 3145736 | tf_op jit(solution)/shard_map/ppermute | solution.py:37
  54.7 15.0 %collective-permute-done.12 = f32[16,8192]{1,0:T(8,128)S(1)} collective-permute-done((f32[16,8192]{1,0:T(8,128)S(1)}, f32[16,8192]{1,0:T(8,128)S(1)}, u32[]{:S(2)}, u32[]{:S(2)}) %collective-permute-start.12) | collective-permute-done | bytes 524320 | tf_op jit(solution)/shard_map/ppermute | solution.py:344
  70.8 3.9 %shard_map.112 = (f32[512,1024]{1,0:T(8,128)S(1)}, bf16[512,4096]{1,0:T(8,128)(2,1)}) custom-call(bf16[512,4096]{1,0:T(8,128)(2,1)S(1)} %copy-done, bf16[512,1024]{1,0:T(8,128)(2,1)S(1)} %copy-done.1, bf16[1024,1024]{1,0:T(8,128)(2,1)S(1)} %shard_map.111.refs_2_), custom_call_target="tpu_custom_call" | custom-call | bytes 1048576 | tf_op jit(solution)/shard_map/pallas_call | solution.py:189
  76.1 3.0 %collective-permute-start.15 = (f16[256,1024]{1,0:T(8,128)(2,1)S(1)}, f16[256,1024]{1,0:T(8,128)(2,1)S(1)}, u32[]{:S(2)}, u32[]{:S(2)}) collective-permute-start(f16[256,1024]{1,0:T(8,128)(2,1)S(1)} %get-tuple-element.93), channel_id=1, source_target_pairs={{0,3},{1,0},{2,1},{3,2},{4,7},{5,4},{6,5},{7,6},{8,11},{9,8},{10,9... | collective-permute-start | bytes 1572872 | tf_op jit(solution)/shard_map/ppermute | solution.py:37
  79.9 1.3 slice.172
  81.2 1.3 slice.173
  83.4 2.4 %collective-permute-start.8 = (bf16[512,1024]{1,0:T(8,128)(2,1)S(1)}, bf16[512,1024]{1,0:T(8,128)(2,1)S(1)}, u32[]{:S(2)}, u32[]{:S(2)}) collective-permute-start(bf16[512,1024]{1,0:T(8,128)(2,1)S(1)} %slice.172), channel_id=1, source_target_pairs={{0,8},{1,9},{2,10},{3,11},{4,12},{5,13},{6,14},{7,15},{8,16},{9,17... | collective-permute-start | bytes 3145736 | tf_op jit(solution)/shard_map/ppermute | solution.py:37
  86.5 1.4 collective-permute-done.15
  87.9 4.0 %collective-permute-done.13 = f16[256,1024]{1,0:T(8,128)(2,1)S(1)} collective-permute-done((f16[256,1024]{1,0:T(8,128)(2,1)S(1)}, f16[256,1024]{1,0:T(8,128)(2,1)S(1)}, u32[]{:S(2)}, u32[]{:S(2)}) %collective-permute-start.13) | collective-permute-done | bytes 524320 | tf_op jit(solution)/shard_map/ppermute | solution.py:37
  94.0 3.0 %collective-permute-start.19 = (f16[144,1024]{1,0:T(8,128)(2,1)S(1)}, f16[144,1024]{1,0:T(8,128)(2,1)S(1)}, u32[]{:S(2)}, u32[]{:S(2)}) collective-permute-start(f16[144,1024]{1,0:T(8,128)(2,1)S(1)} %slice_select_fusion.1), channel_id=1, source_target_pairs={{0,16},{1,17},{2,18},{3,19},{4,20},{5,21},{6,22},{7,23},{8,24},{9,... | collective-permute-start | bytes 884744 | tf_op jit(solution)/shard_map/ppermute | solution.py:37
  98.6 6.4 %collective-permute-start.16 = (f16[512,1024]{1,0:T(8,128)(2,1)S(1)}, f16[512,1024]{1,0:T(8,128)(2,1)S(1)}, u32[]{:S(2)}, u32[]{:S(2)}) collective-permute-start(f16[512,1024]{1,0:T(8,128)(2,1)S(1)} %multiply_convert_fusion.3), channel_id=1, source_target_pairs={{0,3},{1,0},{2,1},{3,2},{4,7},{5,4},{6,5},{7,6},{8,11},{9,8},{10,9... | collective-permute-start | bytes 3145736 | tf_op jit(solution)/shard_map/ppermute | solution.py:37
  106.6 7.4 %shard_map.113 = (f32[512,1024]{1,0:T(8,128)S(1)}, bf16[512,4096]{1,0:T(8,128)(2,1)}) custom-call(bf16[512,4096]{1,0:T(8,128)(2,1)S(1)} %copy-done, bf16[512,1024]{1,0:T(8,128)(2,1)S(1)} %copy-done.1, bf16[1024,1024]{1,0:T(8,128)(2,1)} %collective-permute-done.6.refs_2_, ...), custom_call_target="tpu_custom_call", output_to_operand_aliasing={{1}: (5, {})} | custom-call | bytes 1048576 | tf_op jit(solution)/shard_map/pallas_call | solution.py:189
  114.0 4.3 %collective-permute-done.14 = f16[512,1024]{1,0:T(8,128)(2,1)S(1)} collective-permute-done((f16[512,1024]{1,0:T(8,128)(2,1)S(1)}, f16[512,1024]{1,0:T(8,128)(2,1)S(1)}, u32[]{:S(2)}, u32[]{:S(2)}) %collective-permute-start.14) | collective-permute-done | bytes 1048608 | tf_op jit(solution)/shard_map/ppermute | solution.py:37
  118.8 2.7 %collective-permute-start.21 = (f16[256,1024]{1,0:T(8,128)(2,1)S(1)}, f16[256,1024]{1,0:T(8,128)(2,1)S(1)}, u32[]{:S(2)}, u32[]{:S(2)}) collective-permute-start(f16[256,1024]{1,0:T(8,128)(2,1)S(1)} %get-tuple-element.112), channel_id=1, source_target_pairs={{0,3},{1,0},{2,1},{3,2},{4,7},{5,4},{6,5},{7,6},{8,11},{9,8},{10,9... | collective-permute-start | bytes 1572872 | tf_op jit(solution)/shard_map/ppermute | solution.py:37
  122.3 10.2 %collective-permute-start.25 = (f16[144,1024]{1,0:T(8,128)(2,1)S(1)}, f16[144,1024]{1,0:T(8,128)(2,1)S(1)}, u32[]{:S(2)}, u32[]{:S(2)}) collective-permute-start(f16[144,1024]{1,0:T(8,128)(2,1)S(1)} %pad_maximum_fusion), channel_id=1, source_target_pairs={{0,4},{1,5},{2,6},{3,7},{4,0},{5,1},{6,2},{7,3},{8,12},{9,13},{10,... | collective-permute-start | bytes 884744 | tf_op jit(solution)/shard_map/ppermute | solution.py:37
  132.5 5.0 %shard_map.114 = (bf16[512,1024]{1,0:T(8,128)(2,1)}, bf16[512,4096]{1,0:T(8,128)(2,1)}) custom-call(bf16[512,4096]{1,0:T(8,128)(2,1)S(1)} %copy-done, bf16[512,1024]{1,0:T(8,128)(2,1)S(1)} %copy-done.1, bf16[512,1024]{1,0:T(8,128)(2,1)S(1)} %collective-permute-done.8.refs_2_, ...), custom_call_target="tpu_custom_call", output_to_operand_aliasing={{1}: (5, {})} | custom-call | bytes 1048576 | tf_op jit(solution)/shard_map/pallas_call | solution.py:189
  138.5 4.0 %collective-permute-start.22 = (f16[144,1024]{1,0:T(8,128)(2,1)S(1)}, f16[144,1024]{1,0:T(8,128)(2,1)S(1)}, u32[]{:S(2)}, u32[]{:S(2)}) collective-permute-start(f16[144,1024]{1,0:T(8,128)(2,1)S(1)} %concatenate.29), channel_id=1, source_target_pairs={{0,8},{1,9},{2,10},{3,11},{4,12},{5,13},{6,14},{7,15},{8,16},{9,17... | collective-permute-start | bytes 884744 | tf_op jit(solution)/shard_map/ppermute | solution.py:37
  142.7 1.7 %collective-permute-start.24 = (f16[144,1024]{1,0:T(8,128)(2,1)S(1)}, f16[144,1024]{1,0:T(8,128)(2,1)S(1)}, u32[]{:S(2)}, u32[]{:S(2)}) collective-permute-start(f16[144,1024]{1,0:T(8,128)(2,1)S(1)} %slice_select_fusion), channel_id=1, source_target_pairs={{0,16},{1,17},{2,18},{3,19},{4,20},{5,21},{6,22},{7,23},{8,24},{9,... | collective-permute-start | bytes 884744 | tf_op jit(solution)/shard_map/ppermute | solution.py:37
  144.4 2.3 %collective-permute-done.22 = f16[144,1024]{1,0:T(8,128)(2,1)S(1)} collective-permute-done((f16[144,1024]{1,0:T(8,128)(2,1)S(1)}, f16[144,1024]{1,0:T(8,128)(2,1)S(1)}, u32[]{:S(2)}, u32[]{:S(2)}) %collective-permute-start.22) | collective-permute-done | bytes 294944 | tf_op jit(solution)/shard_map/ppermute | solution.py:37
  146.7 7.1 %collective-permute-done.23 = f16[144,1024]{1,0:T(8,128)(2,1)S(1)} collective-permute-done((f16[144,1024]{1,0:T(8,128)(2,1)S(1)}, f16[144,1024]{1,0:T(8,128)(2,1)S(1)}, u32[]{:S(2)}, u32[]{:S(2)}) %collective-permute-start.23) | collective-permute-done | bytes 294944 | tf_op jit(solution)/shard_map/ppermute | solution.py:37
  (87 shorter events, 20.1 us)
Async XLA Ops:
  2.3 21.0 %collective-permute-start.10 = (f32[16,8192]{1,0:T(8,128)S(1)}, f32[16,8192]{1,0:T(8,128)S(1)}, u32[]{:S(2)}, u32[]{:S(2)}) collective-permute-start(f32[16,8192]{1,0:T(8,128)S(1)} %multiply_bitcast_fusion.1), channel_id=1, source_target_pairs={{0,32},{32,0},{64,96},{96,64},{128,160},{160,128},{192,224},{224,1... | collective-permute-start | bytes 1572872 | tf_op jit(solution)/shard_map/ppermute | solution.py:344
  2.4 15.6 %copy-start.5 = (bf16[1,128,1024]{2,1,0:T(8,128)(2,1)S(1)}, bf16[1,128,1024]{2,1,0:T(8,128)(2,1)}, u32[]{:S(2)}) copy-start(bf16[1,128,1024]{2,1,0:T(8,128)(2,1)} %param.8) | copy-start | bytes 786436
  2.4 20.9 %copy-start.2 = (bf16[1,16,8192]{2,1,0:T(8,128)(2,1)S(1)}, bf16[1,16,8192]{2,1,0:T(8,128)(2,1)}, u32[]{:S(2)}) copy-start(bf16[1,16,8192]{2,1,0:T(8,128)(2,1)} %param.10) | copy-start | bytes 786436
  2.4 15.6 %collective-permute-start = (bf16[128,1024]{1,0:T(8,128)(2,1)}, bf16[128,1024]{1,0:T(8,128)(2,1)S(1)}, u32[]{:S(2)}, u32[]{:S(2)}) collective-permute-start(bf16[128,1024]{1,0:T(8,128)(2,1)} %bitcast.53), channel_id=1, source_target_pairs={{0,4},{1,5},{2,6},{3,7},{4,0},{5,1},{6,2},{7,3},{8,12},{9,13},{10,... | collective-permute-start | bytes 786440 | tf_op jit(solution)/shard_map/ppermute | solution.py:37
  18.1 17.2 %collective-permute-start.3 = (bf16[272,1024]{1,0:T(8,128)(2,1)S(1)}, bf16[272,1024]{1,0:T(8,128)(2,1)S(1)}, u32[]{:S(2)}, u32[]{:S(2)}) collective-permute-start(bf16[272,1024]{1,0:T(8,128)(2,1)S(1)} %maximum_maximum_fusion.refs_0_), channel_id=1, source_target_pairs={{0,2},{1,3},{2,0},{3,1},{4,6},{5,7},{6,4},{7,5},{8,10},{9,11},{10,... | collective-permute-start | bytes 1671176 | tf_op jit(solution)/shard_map/ppermute | solution.py:37
  21.2 14.1 %collective-permute-start.2 = (bf16[272,1024]{1,0:T(8,128)(2,1)S(1)}, bf16[272,1024]{1,0:T(8,128)(2,1)S(1)}, u32[]{:S(2)}, u32[]{:S(2)}) collective-permute-start(bf16[272,1024]{1,0:T(8,128)(2,1)S(1)} %maximum_maximum_fusion.refs_0_), channel_id=1, source_target_pairs={{0,3},{1,0},{2,1},{3,2},{4,7},{5,4},{6,5},{7,6},{8,11},{9,8},{10,9... | collective-permute-start | bytes 1671176 | tf_op jit(solution)/shard_map/ppermute | solution.py:37
  22.4 13.0 %collective-permute-start.1 = (bf16[272,1024]{1,0:T(8,128)(2,1)S(1)}, bf16[272,1024]{1,0:T(8,128)(2,1)S(1)}, u32[]{:S(2)}, u32[]{:S(2)}) collective-permute-start(bf16[272,1024]{1,0:T(8,128)(2,1)S(1)} %maximum_maximum_fusion.refs_0_), channel_id=1, source_target_pairs={{0,1},{1,2},{2,3},{3,0},{4,5},{5,6},{6,7},{7,4},{8,9},{9,10},{10,1... | collective-permute-start | bytes 1671176 | tf_op jit(solution)/shard_map/ppermute | solution.py:37
  24.1 16.8 %collective-permute-start.11 = (f32[16,8192]{1,0:T(8,128)}, f32[16,8192]{1,0:T(8,128)}, u32[]{:S(2)}, u32[]{:S(2)}) collective-permute-start(f32[16,8192]{1,0:T(8,128)} %fusion.16), channel_id=1, source_target_pairs={{0,64},{32,96},{64,0},{96,32},{128,192},{160,224},{192,128},{224,1... | collective-permute-start | bytes 1572872 | tf_op jit(solution)/shard_map/ppermute | solution.py:344
  29.7 19.1 %copy-start.1 = (bf16[512,1024]{1,0:T(8,128)(2,1)S(1)}, bf16[512,1024]{1,0:T(8,128)(2,1)}, u32[]{:S(2)}) copy-start(bf16[512,1024]{1,0:T(8,128)(2,1)} %refs_1_.2) | copy-start | bytes 3145732
  35.6 40.5 %collective-permute-start.7 = (bf16[1024,1024]{1,0:T(8,128)(2,1)S(1)}, bf16[1024,1024]{1,0:T(8,128)(2,1)}, u32[]{:S(2)}, u32[]{:S(2)}) collective-permute-start(bf16[1024,1024]{1,0:T(8,128)(2,1)S(1)} %shard_map.111.refs_2_), channel_id=1, source_target_pairs={{0,24},{1,25},{2,26},{3,27},{4,28},{5,29},{6,30},{7,31},{8,0},{9,1... | collective-permute-start | bytes 6291464 | tf_op jit(solution)/shard_map/ppermute | solution.py:37
  36.4 39.7 %collective-permute-start.6 = (bf16[1024,1024]{1,0:T(8,128)(2,1)S(1)}, bf16[1024,1024]{1,0:T(8,128)(2,1)}, u32[]{:S(2)}, u32[]{:S(2)}) collective-permute-start(bf16[1024,1024]{1,0:T(8,128)(2,1)S(1)} %shard_map.111.refs_2_), channel_id=1, source_target_pairs={{0,8},{1,9},{2,10},{3,11},{4,12},{5,13},{6,14},{7,15},{8,16},{9,17... | collective-permute-start | bytes 6291464 | tf_op jit(solution)/shard_map/ppermute | solution.py:37
  42.3 27.4 %collective-permute-start.12 = (f32[16,8192]{1,0:T(8,128)S(1)}, f32[16,8192]{1,0:T(8,128)S(1)}, u32[]{:S(2)}, u32[]{:S(2)}) collective-permute-start(f32[16,8192]{1,0:T(8,128)S(1)} %add.81), channel_id=1, source_target_pairs={{0,128},{32,160},{64,192},{96,224},{128,0},{160,32},{192,64},{224,... | collective-permute-start | bytes 1572872 | tf_op jit(solution)/shard_map/ppermute | solution.py:344
  48.8 20.9 %copy-start.3 = (f32[16,8192]{1,0:T(8,128)S(1)}, f32[16,8192]{1,0:T(8,128)}, u32[]{:S(2)}) copy-start(f32[16,8192]{1,0:T(8,128)} %param.12) | copy-start | bytes 1572868
  48.8 21.0 %copy-start.4 = (f32[16,8192]{1,0:T(8,128)S(1)}, f32[16,8192]{1,0:T(8,128)}, u32[]{:S(2)}) copy-start(f32[16,8192]{1,0:T(8,128)} %param.13) | copy-start | bytes 1572868
  50.7 20.2 %copy-start = (bf16[512,4096]{1,0:T(8,128)(2,1)S(1)}, bf16[512,4096]{1,0:T(8,128)(2,1)}, u32[]{:S(2)}) copy-start(bf16[512,4096]{1,0:T(8,128)(2,1)} %refs_0_.5) | copy-start | bytes 12582916
  51.4 24.1 %collective-permute-start.4 = (f16[512,1024]{1,0:T(8,128)(2,1)S(1)}, f16[512,1024]{1,0:T(8,128)(2,1)S(1)}, u32[]{:S(2)}, u32[]{:S(2)}) collective-permute-start(f16[512,1024]{1,0:T(8,128)(2,1)S(1)} %multiply_convert_fusion.7), channel_id=1, source_target_pairs={{0,1},{1,2},{2,3},{3,0},{4,5},{5,6},{6,7},{7,4},{8,9},{9,10},{10,1... | collective-permute-start | bytes 3145736 | tf_op jit(solution)/shard_map/ppermute | solution.py:37
  52.9 22.6 %collective-permute-start.5 = (f16[512,1024]{1,0:T(8,128)(2,1)S(1)}, f16[512,1024]{1,0:T(8,128)(2,1)S(1)}, u32[]{:S(2)}, u32[]{:S(2)}) collective-permute-start(f16[512,1024]{1,0:T(8,128)(2,1)S(1)} %multiply_convert_fusion.6), channel_id=1, source_target_pairs={{0,3},{1,0},{2,1},{3,2},{4,7},{5,4},{6,5},{7,6},{8,11},{9,8},{10,9... | collective-permute-start | bytes 3145736 | tf_op jit(solution)/shard_map/ppermute | solution.py:37
  76.1 11.8 %collective-permute-start.15 = (f16[256,1024]{1,0:T(8,128)(2,1)S(1)}, f16[256,1024]{1,0:T(8,128)(2,1)S(1)}, u32[]{:S(2)}, u32[]{:S(2)}) collective-permute-start(f16[256,1024]{1,0:T(8,128)(2,1)S(1)} %get-tuple-element.93), channel_id=1, source_target_pairs={{0,3},{1,0},{2,1},{3,2},{4,7},{5,4},{6,5},{7,6},{8,11},{9,8},{10,9... | collective-permute-start | bytes 1572872 | tf_op jit(solution)/shard_map/ppermute | solution.py:37
  79.1 12.8 %collective-permute-start.13 = (f16[256,1024]{1,0:T(8,128)(2,1)S(1)}, f16[256,1024]{1,0:T(8,128)(2,1)S(1)}, u32[]{:S(2)}, u32[]{:S(2)}) collective-permute-start(f16[256,1024]{1,0:T(8,128)(2,1)S(1)} %get-tuple-element.89), channel_id=1, source_target_pairs={{0,1},{1,2},{2,3},{3,0},{4,5},{5,6},{6,7},{7,4},{8,9},{9,10},{10,1... | collective-permute-start | bytes 1572872 | tf_op jit(solution)/shard_map/ppermute | solution.py:37
  82.5 16.1 %collective-permute-start.9 = (bf16[512,1024]{1,0:T(8,128)(2,1)S(1)}, bf16[512,1024]{1,0:T(8,128)(2,1)S(1)}, u32[]{:S(2)}, u32[]{:S(2)}) collective-permute-start(bf16[512,1024]{1,0:T(8,128)(2,1)S(1)} %slice.173), channel_id=1, source_target_pairs={{0,24},{1,25},{2,26},{3,27},{4,28},{5,29},{6,30},{7,31},{8,0},{9,1... | collective-permute-start | bytes 3145736 | tf_op jit(solution)/shard_map/ppermute | solution.py:37
  83.4 15.2 %collective-permute-start.8 = (bf16[512,1024]{1,0:T(8,128)(2,1)S(1)}, bf16[512,1024]{1,0:T(8,128)(2,1)S(1)}, u32[]{:S(2)}, u32[]{:S(2)}) collective-permute-start(bf16[512,1024]{1,0:T(8,128)(2,1)S(1)} %slice.172), channel_id=1, source_target_pairs={{0,8},{1,9},{2,10},{3,11},{4,12},{5,13},{6,14},{7,15},{8,16},{9,17... | collective-permute-start | bytes 3145736 | tf_op jit(solution)/shard_map/ppermute | solution.py:37
  92.9 12.8 %collective-permute-start.17 = (f16[144,1024]{1,0:T(8,128)(2,1)S(1)}, f16[144,1024]{1,0:T(8,128)(2,1)S(1)}, u32[]{:S(2)}, u32[]{:S(2)}) collective-permute-start(f16[144,1024]{1,0:T(8,128)(2,1)S(1)} %concatenate.25), channel_id=1, source_target_pairs={{0,8},{1,9},{2,10},{3,11},{4,12},{5,13},{6,14},{7,15},{8,16},{9,17... | collective-permute-start | bytes 884744 | tf_op jit(solution)/shard_map/ppermute | solution.py:37
  94.0 12.1 %collective-permute-start.19 = (f16[144,1024]{1,0:T(8,128)(2,1)S(1)}, f16[144,1024]{1,0:T(8,128)(2,1)S(1)}, u32[]{:S(2)}, u32[]{:S(2)}) collective-permute-start(f16[144,1024]{1,0:T(8,128)(2,1)S(1)} %slice_select_fusion.1), channel_id=1, source_target_pairs={{0,16},{1,17},{2,18},{3,19},{4,20},{5,21},{6,22},{7,23},{8,24},{9,... | collective-permute-start | bytes 884744 | tf_op jit(solution)/shard_map/ppermute | solution.py:37
  97.0 9.1 %collective-permute-start.18 = (f16[144,1024]{1,0:T(8,128)(2,1)S(1)}, f16[144,1024]{1,0:T(8,128)(2,1)S(1)}, u32[]{:S(2)}, u32[]{:S(2)}) collective-permute-start(f16[144,1024]{1,0:T(8,128)(2,1)S(1)} %concatenate.26), channel_id=1, source_target_pairs={{0,24},{1,25},{2,26},{3,27},{4,28},{5,29},{6,30},{7,31},{8,0},{9,1... | collective-permute-start | bytes 884744 | tf_op jit(solution)/shard_map/ppermute | solution.py:37
  98.5 19.7 %collective-permute-start.14 = (f16[512,1024]{1,0:T(8,128)(2,1)S(1)}, f16[512,1024]{1,0:T(8,128)(2,1)S(1)}, u32[]{:S(2)}, u32[]{:S(2)}) collective-permute-start(f16[512,1024]{1,0:T(8,128)(2,1)S(1)} %multiply_convert_fusion.4), channel_id=1, source_target_pairs={{0,1},{1,2},{2,3},{3,0},{4,5},{5,6},{6,7},{7,4},{8,9},{9,10},{10,1... | collective-permute-start | bytes 3145736 | tf_op jit(solution)/shard_map/ppermute | solution.py:37
  98.6 19.7 %collective-permute-start.16 = (f16[512,1024]{1,0:T(8,128)(2,1)S(1)}, f16[512,1024]{1,0:T(8,128)(2,1)S(1)}, u32[]{:S(2)}, u32[]{:S(2)}) collective-permute-start(f16[512,1024]{1,0:T(8,128)(2,1)S(1)} %multiply_convert_fusion.3), channel_id=1, source_target_pairs={{0,3},{1,0},{2,1},{3,2},{4,7},{5,4},{6,5},{7,6},{8,11},{9,8},{10,9... | collective-permute-start | bytes 3145736 | tf_op jit(solution)/shard_map/ppermute | solution.py:37
  118.8 18.7 %collective-permute-start.21 = (f16[256,1024]{1,0:T(8,128)(2,1)S(1)}, f16[256,1024]{1,0:T(8,128)(2,1)S(1)}, u32[]{:S(2)}, u32[]{:S(2)}) collective-permute-start(f16[256,1024]{1,0:T(8,128)(2,1)S(1)} %get-tuple-element.112), channel_id=1, source_target_pairs={{0,3},{1,0},{2,1},{3,2},{4,7},{5,4},{6,5},{7,6},{8,11},{9,8},{10,9... | collective-permute-start | bytes 1572872 | tf_op jit(solution)/shard_map/ppermute | solution.py:37
  121.5 16.0 %collective-permute-start.20 = (f16[256,1024]{1,0:T(8,128)(2,1)S(1)}, f16[256,1024]{1,0:T(8,128)(2,1)S(1)}, u32[]{:S(2)}, u32[]{:S(2)}) collective-permute-start(f16[256,1024]{1,0:T(8,128)(2,1)S(1)} %get-tuple-element.111), channel_id=1, source_target_pairs={{0,1},{1,2},{2,3},{3,0},{4,5},{5,6},{6,7},{7,4},{8,9},{9,10},{10,1... | collective-permute-start | bytes 1572872 | tf_op jit(solution)/shard_map/ppermute | solution.py:37
  122.3 22.1 %collective-permute-start.25 = (f16[144,1024]{1,0:T(8,128)(2,1)S(1)}, f16[144,1024]{1,0:T(8,128)(2,1)S(1)}, u32[]{:S(2)}, u32[]{:S(2)}) collective-permute-start(f16[144,1024]{1,0:T(8,128)(2,1)S(1)} %pad_maximum_fusion), channel_id=1, source_target_pairs={{0,4},{1,5},{2,6},{3,7},{4,0},{5,1},{6,2},{7,3},{8,12},{9,13},{10,... | collective-permute-start | bytes 884744 | tf_op jit(solution)/shard_map/ppermute | solution.py:37
  138.5 8.2 %collective-permute-start.22 = (f16[144,1024]{1,0:T(8,128)(2,1)S(1)}, f16[144,1024]{1,0:T(8,128)(2,1)S(1)}, u32[]{:S(2)}, u32[]{:S(2)}) collective-permute-start(f16[144,1024]{1,0:T(8,128)(2,1)S(1)} %concatenate.29), channel_id=1, source_target_pairs={{0,8},{1,9},{2,10},{3,11},{4,12},{5,13},{6,14},{7,15},{8,16},{9,17... | collective-permute-start | bytes 884744 | tf_op jit(solution)/shard_map/ppermute | solution.py:37
  142.6 11.2 %collective-permute-start.23 = (f16[144,1024]{1,0:T(8,128)(2,1)S(1)}, f16[144,1024]{1,0:T(8,128)(2,1)S(1)}, u32[]{:S(2)}, u32[]{:S(2)}) collective-permute-start(f16[144,1024]{1,0:T(8,128)(2,1)S(1)} %concatenate.30), channel_id=1, source_target_pairs={{0,24},{1,25},{2,26},{3,27},{4,28},{5,29},{6,30},{7,31},{8,0},{9,1... | collective-permute-start | bytes 884744 | tf_op jit(solution)/shard_map/ppermute | solution.py:37
  142.7 11.1 %collective-permute-start.24 = (f16[144,1024]{1,0:T(8,128)(2,1)S(1)}, f16[144,1024]{1,0:T(8,128)(2,1)S(1)}, u32[]{:S(2)}, u32[]{:S(2)}) collective-permute-start(f16[144,1024]{1,0:T(8,128)(2,1)S(1)} %slice_select_fusion), channel_id=1, source_target_pairs={{0,16},{1,17},{2,18},{3,19},{4,20},{5,21},{6,22},{7,23},{8,24},{9,... | collective-permute-start | bytes 884744 | tf_op jit(solution)/shard_map/ppermute | solution.py:37
  (2 other events, 11.0 us)

commit v2 on v1

--- a/solution.py
+++ b/solution.py
@@ -267,10 +267,12 @@
 
 def gather_u(lanes, near, far, note):
     n = near.shape[0]
-    own = jnp.concatenate([near, far, note], axis=0)
+    own = jnp.concatenate([near, note], axis=0)
     f, o, b = all_of_ring(lanes, "u", own, own, own)
-    row = join((own, f, o, b), [(m, p * n, n) for pair in ((0, 1), (2, 3)) for p in range(NZ) for m in pair])
-    notes = [x[2 * n :, :128].astype(F32) for x in (own, f, o, b)]
+    far = after(far, f, o, b)
+    far_f, far_o, far_b = all_of_ring(lanes, "u", far, far, far, "far ")
+    row = join((near, f, far, far_f, o, b, far_o, far_b), [(m, 0, n) for m in range(2 * NX)])
+    notes = [x[n:, :128].astype(F32) for x in (own, f, o, b)]
     return row, jnp.maximum(jnp.maximum(notes[0], notes[1]), jnp.maximum(notes[2], notes[3]))
 
 

time: 156 us -> 166 us (1.064)
  waiting for transfers between devices: 43.2 us -> 56.8 us
  local copies, waits for them, and re-layouts: 3.71 us -> 1.26 us
  other arithmetic: 9.8 us -> 7.58 us
    ppermute x23 -> x26, waiting for transfers between devices: 28.2 us -> 40.9 us  [move(): return lax.ppermute(a, ('rep', 'fsdp'), pairs)]
    ppermute x23 -> x26, starting transfers between devices: 54.4 us -> 63.1 us  [move(): return lax.ppermute(a, ('rep', 'fsdp'), pairs)]
    ppermute x3, starting transfers between devices: 12.1 us -> 4.19 us  [sum_of_replicas(): lax.ppermute(a, 'rep', pairs)]
    slice x2, local copies, waits for them, and re-layouts: 2.59 us -> 0.14 us  [gather_v(): low, high = lanes.both('v', f[:LOW], b[LOW:])]
    add x2, other arithmetic: 2.25 us -> 0.11 us  [sum_of_replicas(): total + lanes.queue('r', total, lambda a: lax.ppermute(a, 'rep', pairs))]
  transfers between devices with their start and end apart: 26 -> 29, of which waited for: 10 -> 13; matrix products, arithmetic and copies ran while one was open for 12% -> 7% of each run, Pallas kernels for 14% -> 13%
where the time goes in v2:
time: 166 us; the launch traced here: 163 us
  starting transfers between devices  67.3 us (41%)
  waiting for transfers between devices  56.8 us (34%)
  Pallas kernels  21.2 us (13%)
  other arithmetic  7.58 us (5%)
  matrix products  5.83 us (4%)
  between operations  3.34 us (2%)
    ppermute x26, starting transfers between devices, move(): return lax.ppermute(a, ('rep', 'fsdp'), pairs)  63.1 us
    ppermute x26, waiting for transfers between devices, move(): return lax.ppermute(a, ('rep', 'fsdp'), pairs)  40.9 us
    pallas_call x3, Pallas kernels, products(): pl.pallas_call(lambda *refs: product_kernel(counts, bool(before), *refs),...  16 us
    ppermute x3, waiting for transfers between devices, sum_of_replicas(): lax.ppermute(a, 'rep', pairs)  15.9 us
    dot_general x8, matrix products, terms(): g = jnp.einsum('td,tk->dk', part, cot, preferred_element_type=F32)  5.83 us
    pallas_call x1, Pallas kernels, sort(): pl.pallas_call(sort_kernel, in_specs=[any_, any_], out_specs=[any_, pl.Bl...  4.97 us
    ppermute x3, starting transfers between devices, sum_of_replicas(): lax.ppermute(a, 'rep', pairs)  4.19 us
  transfers between devices with their start and end apart: 29, of which 13 were waited for; matrix products, arithmetic and copies ran while one was open for 7% of the time, Pallas kernels for 13%

profile of v2, /device:TPU:24, one launch (start us, length us, event | category | flops | bytes accessed | tf_op | source)
XLA Modules:
  0.0 163.4 jit_solution(712434329836941686)
XLA Ops:
  2.4 7.3 %collective-permute-start.3 = (bf16[128,1024]{1,0:T(8,128)(2,1)}, bf16[128,1024]{1,0:T(8,128)(2,1)S(1)}, u32[]{:S(2)}, u32[]{:S(2)}) collective-permute-start(bf16[128,1024]{1,0:T(8,128)(2,1)} %bitcast.53), channel_id=1, source_target_pairs={{0,4},{1,5},{2,6},{3,7},{4,0},{5,1},{6,2},{7,3},{8,12},{9,13},{10,... | collective-permute-start | bytes 786440 | tf_op jit(solution)/shard_map/ppermute | solution.py:37
  9.7 5.0 %shard_map.110 = (bf16[2,4,512,512]{3,2,1,0:T(8,128)(2,1)}, f32[2,8,128]{2,1,0:T(8,128)}) custom-call(bf16[512,4096]{1,0:T(8,128)(2,1)} %refs_0_.5, bf16[512,1024]{1,0:T(8,128)(2,1)} %refs_1_.2), custom_call_target="tpu_custom_call" | custom-call | bytes 1048576 | tf_op jit(solution)/shard_map/pallas_call | solution.py:105
  15.8 3.1 %collective-permute-start.2 = (bf16[144,1024]{1,0:T(8,128)(2,1)S(1)}, bf16[144,1024]{1,0:T(8,128)(2,1)S(1)}, u32[]{:S(2)}, u32[]{:S(2)}) collective-permute-start(bf16[144,1024]{1,0:T(8,128)(2,1)S(1)} %pad_maximum_fusion), channel_id=1, source_target_pairs={{0,2},{1,3},{2,0},{3,1},{4,6},{5,7},{6,4},{7,5},{8,10},{9,11},{10,... | collective-permute-start | bytes 884744 | tf_op jit(solution)/shard_map/ppermute | solution.py:37
  21.0 2.6 %collective-permute-start.14 = (f32[16,8192]{1,0:T(8,128)S(1)}, f32[16,8192]{1,0:T(8,128)S(1)}, u32[]{:S(2)}, u32[]{:S(2)}) collective-permute-start(f32[16,8192]{1,0:T(8,128)S(1)} %fusion.16), channel_id=1, source_target_pairs={{0,64},{32,96},{64,0},{96,32},{128,192},{160,224},{192,128},{224,1... | collective-permute-start | bytes 1572872 | tf_op jit(solution)/shard_map/ppermute | solution.py:346
  23.5 3.8 %collective-permute-done.1.refs_5_ = bf16[144,1024]{1,0:T(8,128)(2,1)S(1)} collective-permute-done((bf16[144,1024]{1,0:T(8,128)(2,1)S(1)}, bf16[144,1024]{1,0:T(8,128)(2,1)S(1)}, u32[]{:S(2)}, u32[]{:S(2)}) %collective-permute-start.1) | collective-permute-done | bytes 294944 | tf_op jit(solution)/shard_map/ppermute | solution.py:37
  28.0 2.3 %collective-permute-start.6 = (bf16[128,1024]{1,0:T(8,128)(2,1)S(1)}, bf16[128,1024]{1,0:T(8,128)(2,1)S(1)}, u32[]{:S(2)}, u32[]{:S(2)}) collective-permute-start(bf16[128,1024]{1,0:T(8,128)(2,1)S(1)} %collective-permute-done.3.refs_2_), channel_id=1, source_target_pairs={{0,2},{1,3},{2,0},{3,1},{4,6},{5,7},{6,4},{7,5},{8,10},{9,11},{10,... | collective-permute-start | bytes 786440 | tf_op jit(solution)/shard_map/ppermute | solution.py:37
  30.3 1.2 collective-permute-start.5
  34.3 3.7 %collective-permute-done.5.refs_7_ = bf16[128,1024]{1,0:T(8,128)(2,1)S(1)} collective-permute-done((bf16[128,1024]{1,0:T(8,128)(2,1)S(1)}, bf16[128,1024]{1,0:T(8,128)(2,1)S(1)}, u32[]{:S(2)}, u32[]{:S(2)}) %collective-permute-start.5) | collective-permute-done | bytes 262176 | tf_op jit(solution)/shard_map/ppermute | solution.py:37
  40.1 2.5 %collective-permute-start.9 = (bf16[1024,1024]{1,0:T(8,128)(2,1)S(1)}, bf16[1024,1024]{1,0:T(8,128)(2,1)S(1)}, u32[]{:S(2)}, u32[]{:S(2)}) collective-permute-start(bf16[1024,1024]{1,0:T(8,128)(2,1)S(1)} %shard_map.111.refs_2_), channel_id=1, source_target_pairs={{0,8},{1,9},{2,10},{3,11},{4,12},{5,13},{6,14},{7,15},{8,16},{9,17... | collective-permute-start | bytes 6291464 | tf_op jit(solution)/shard_map/ppermute | solution.py:37
  42.7 1.5 collective-permute-start.15
  46.3 3.0 %collective-permute-start.8 = (f16[512,1024]{1,0:T(8,128)(2,1)S(1)}, f16[512,1024]{1,0:T(8,128)(2,1)S(1)}, u32[]{:S(2)}, u32[]{:S(2)}) collective-permute-start(f16[512,1024]{1,0:T(8,128)(2,1)S(1)} %multiply_convert_fusion.6), channel_id=1, source_target_pairs={{0,3},{1,0},{2,1},{3,2},{4,7},{5,4},{6,5},{7,6},{8,11},{9,8},{10,9... | collective-permute-start | bytes 3145736 | tf_op jit(solution)/shard_map/ppermute | solution.py:37
  49.3 15.9 %collective-permute-done.15 = f32[16,8192]{1,0:T(8,128)S(1)} collective-permute-done((f32[16,8192]{1,0:T(8,128)S(1)}, f32[16,8192]{1,0:T(8,128)S(1)}, u32[]{:S(2)}, u32[]{:S(2)}) %collective-permute-start.15) | collective-permute-done | bytes 524320 | tf_op jit(solution)/shard_map/ppermute | solution.py:346
  66.3 3.9 %shard_map.112 = (f32[512,1024]{1,0:T(8,128)S(1)}, bf16[512,4096]{1,0:T(8,128)(2,1)}) custom-call(bf16[512,4096]{1,0:T(8,128)(2,1)S(1)} %copy-done, bf16[512,1024]{1,0:T(8,128)(2,1)S(1)} %copy-done.1, bf16[1024,1024]{1,0:T(8,128)(2,1)S(1)} %shard_map.111.refs_2_), custom_call_target="tpu_custom_call" | custom-call | bytes 1048576 | tf_op jit(solution)/shard_map/pallas_call | solution.py:189
  71.0 2.1 %collective-permute-done.7 = f16[512,1024]{1,0:T(8,128)(2,1)S(1)} collective-permute-done((f16[512,1024]{1,0:T(8,128)(2,1)S(1)}, f16[512,1024]{1,0:T(8,128)(2,1)S(1)}, u32[]{:S(2)}, u32[]{:S(2)}) %collective-permute-start.7) | collective-permute-done | bytes 1048608 | tf_op jit(solution)/shard_map/ppermute | solution.py:37
  73.6 4.2 %collective-permute-done.10.refs_3_ = bf16[1024,1024]{1,0:T(8,128)(2,1)S(1)} collective-permute-done((bf16[1024,1024]{1,0:T(8,128)(2,1)S(1)}, bf16[1024,1024]{1,0:T(8,128)(2,1)S(1)}, u32[]{:S(2)}, u32[]{:S(2)}) %collective-permute-start.10) | collective-permute-done | bytes 2097184 | tf_op jit(solution)/shard_map/ppermute | solution.py:37
  77.9 1.6 collective-permute-start.18
  80.9 3.2 %collective-permute-start.11 = (bf16[512,1024]{1,0:T(8,128)(2,1)S(1)}, bf16[512,1024]{1,0:T(8,128)(2,1)S(1)}, u32[]{:S(2)}, u32[]{:S(2)}) collective-permute-start(bf16[512,1024]{1,0:T(8,128)(2,1)S(1)} %slice.172), channel_id=1, source_target_pairs={{0,8},{1,9},{2,10},{3,11},{4,12},{5,13},{6,14},{7,15},{8,16},{9,17... | collective-permute-start | bytes 3145736 | tf_op jit(solution)/shard_map/ppermute | solution.py:37
  84.8 6.8 %collective-permute-done.18 = f16[256,1024]{1,0:T(8,128)(2,1)S(1)} collective-permute-done((f16[256,1024]{1,0:T(8,128)(2,1)S(1)}, f16[256,1024]{1,0:T(8,128)(2,1)S(1)}, u32[]{:S(2)}, u32[]{:S(2)}) %collective-permute-start.18) | collective-permute-done | bytes 524320 | tf_op jit(solution)/shard_map/ppermute | solution.py:37
  91.6 3.9 %collective-permute-done.16 = f16[256,1024]{1,0:T(8,128)(2,1)S(1)} collective-permute-done((f16[256,1024]{1,0:T(8,128)(2,1)S(1)}, f16[256,1024]{1,0:T(8,128)(2,1)S(1)}, u32[]{:S(2)}, u32[]{:S(2)}) %collective-permute-start.16) | collective-permute-done | bytes 524320 | tf_op jit(solution)/shard_map/ppermute | solution.py:37
  96.5 3.4 %collective-permute-start.20 = (f16[144,1024]{1,0:T(8,128)(2,1)S(1)}, f16[144,1024]{1,0:T(8,128)(2,1)S(1)}, u32[]{:S(2)}, u32[]{:S(2)}) collective-permute-start(f16[144,1024]{1,0:T(8,128)(2,1)S(1)} %concatenate.25), channel_id=1, source_target_pairs={{0,8},{1,9},{2,10},{3,11},{4,12},{5,13},{6,14},{7,15},{8,16},{9,17... | collective-permute-start | bytes 884744 | tf_op jit(solution)/shard_map/ppermute | solution.py:37
  102.2 13.1 %collective-permute-start.19 = (f16[512,1024]{1,0:T(8,128)(2,1)S(1)}, f16[512,1024]{1,0:T(8,128)(2,1)S(1)}, u32[]{:S(2)}, u32[]{:S(2)}) collective-permute-start(f16[512,1024]{1,0:T(8,128)(2,1)S(1)} %multiply_convert_fusion.3), channel_id=1, source_target_pairs={{0,3},{1,0},{2,1},{3,2},{4,7},{5,4},{6,5},{7,6},{8,11},{9,8},{10,9... | collective-permute-start | bytes 3145736 | tf_op jit(solution)/shard_map/ppermute | solution.py:37
  116.4 7.1 %shard_map.113 = (f32[512,1024]{1,0:T(8,128)S(1)}, bf16[512,4096]{1,0:T(8,128)(2,1)}) custom-call(bf16[512,4096]{1,0:T(8,128)(2,1)S(1)} %copy-done, bf16[512,1024]{1,0:T(8,128)(2,1)S(1)} %copy-done.1, bf16[1024,1024]{1,0:T(8,128)(2,1)S(1)} %collective-permute-done.9.refs_2_, ...), custom_call_target="tpu_custom_call", output_to_operand_aliasing={{1}: (5, {})} | custom-call | bytes 1048576 | tf_op jit(solution)/shard_map/pallas_call | solution.py:189
  123.6 4.0 %collective-permute-done.19 = f16[512,1024]{1,0:T(8,128)(2,1)S(1)} collective-permute-done((f16[512,1024]{1,0:T(8,128)(2,1)S(1)}, f16[512,1024]{1,0:T(8,128)(2,1)S(1)}, u32[]{:S(2)}, u32[]{:S(2)}) %collective-permute-start.19) | collective-permute-done | bytes 1048608 | tf_op jit(solution)/shard_map/ppermute | solution.py:37
  128.1 3.8 %collective-permute-start.24 = (f16[256,1024]{1,0:T(8,128)(2,1)S(1)}, f16[256,1024]{1,0:T(8,128)(2,1)S(1)}, u32[]{:S(2)}, u32[]{:S(2)}) collective-permute-start(f16[256,1024]{1,0:T(8,128)(2,1)S(1)} %get-tuple-element.118), channel_id=1, source_target_pairs={{0,3},{1,0},{2,1},{3,2},{4,7},{5,4},{6,5},{7,6},{8,11},{9,8},{10,9... | collective-permute-start | bytes 1572872 | tf_op jit(solution)/shard_map/ppermute | solution.py:37
  132.6 1.9 %collective-permute-start.28 = (f16[144,1024]{1,0:T(8,128)(2,1)S(1)}, f16[144,1024]{1,0:T(8,128)(2,1)S(1)}, u32[]{:S(2)}, u32[]{:S(2)}) collective-permute-start(f16[144,1024]{1,0:T(8,128)(2,1)S(1)} %pad_maximum_fusion.1), channel_id=1, source_target_pairs={{0,4},{1,5},{2,6},{3,7},{4,0},{5,1},{6,2},{7,3},{8,12},{9,13},{10,... | collective-permute-start | bytes 884744 | tf_op jit(solution)/shard_map/ppermute | solution.py:37
  134.5 5.0 %shard_map.114 = (bf16[512,1024]{1,0:T(8,128)(2,1)}, bf16[512,4096]{1,0:T(8,128)(2,1)}) custom-call(bf16[512,4096]{1,0:T(8,128)(2,1)S(1)} %copy-done, bf16[512,1024]{1,0:T(8,128)(2,1)S(1)} %copy-done.1, bf16[512,1024]{1,0:T(8,128)(2,1)S(1)} %collective-permute-done.11.refs_2_, ...), custom_call_target="tpu_custom_call", output_to_operand_aliasing={{1}: (5, {})} | custom-call | bytes 1048576 | tf_op jit(solution)/shard_map/pallas_call | solution.py:189
  139.5 3.0 %collective-permute-done.23 = f16[256,1024]{1,0:T(8,128)(2,1)S(1)} collective-permute-done((f16[256,1024]{1,0:T(8,128)(2,1)S(1)}, f16[256,1024]{1,0:T(8,128)(2,1)S(1)}, u32[]{:S(2)}, u32[]{:S(2)}) %collective-permute-start.23) | collective-permute-done | bytes 524320 | tf_op jit(solution)/shard_map/ppermute | solution.py:37
  143.5 2.1 %collective-permute-start.25 = (f16[144,1024]{1,0:T(8,128)(2,1)S(1)}, f16[144,1024]{1,0:T(8,128)(2,1)S(1)}, u32[]{:S(2)}, u32[]{:S(2)}) collective-permute-start(f16[144,1024]{1,0:T(8,128)(2,1)S(1)} %concatenate.29), channel_id=1, source_target_pairs={{0,8},{1,9},{2,10},{3,11},{4,12},{5,13},{6,14},{7,15},{8,16},{9,17... | collective-permute-start | bytes 884744 | tf_op jit(solution)/shard_map/ppermute | solution.py:37
  145.7 6.4 %collective-permute-start.26 = (f16[144,1024]{1,0:T(8,128)(2,1)S(1)}, f16[144,1024]{1,0:T(8,128)(2,1)S(1)}, u32[]{:S(2)}, u32[]{:S(2)}) collective-permute-start(f16[144,1024]{1,0:T(8,128)(2,1)S(1)} %concatenate.30), channel_id=1, source_target_pairs={{0,24},{1,25},{2,26},{3,27},{4,28},{5,29},{6,30},{7,31},{8,0},{9,1... | collective-permute-start | bytes 884744 | tf_op jit(solution)/shard_map/ppermute | solution.py:37
  152.1 2.2 %collective-permute-start.27 = (f16[144,1024]{1,0:T(8,128)(2,1)S(1)}, f16[144,1024]{1,0:T(8,128)(2,1)S(1)}, u32[]{:S(2)}, u32[]{:S(2)}) collective-permute-start(f16[144,1024]{1,0:T(8,128)(2,1)S(1)} %slice_select_fusion), channel_id=1, source_target_pairs={{0,16},{1,17},{2,18},{3,19},{4,20},{5,21},{6,22},{7,23},{8,24},{9,... | collective-permute-start | bytes 884744 | tf_op jit(solution)/shard_map/ppermute | solution.py:37
  154.3 2.3 %collective-permute-done.25 = f16[144,1024]{1,0:T(8,128)(2,1)S(1)} collective-permute-done((f16[144,1024]{1,0:T(8,128)(2,1)S(1)}, f16[144,1024]{1,0:T(8,128)(2,1)S(1)}, u32[]{:S(2)}, u32[]{:S(2)}) %collective-permute-start.25) | collective-permute-done | bytes 294944 | tf_op jit(solution)/shard_map/ppermute | solution.py:37
  156.6 5.4 %collective-permute-done.27 = f16[144,1024]{1,0:T(8,128)(2,1)S(1)} collective-permute-done((f16[144,1024]{1,0:T(8,128)(2,1)S(1)}, f16[144,1024]{1,0:T(8,128)(2,1)S(1)}, u32[]{:S(2)}, u32[]{:S(2)}) %collective-permute-start.27) | collective-permute-done | bytes 294944 | tf_op jit(solution)/shard_map/ppermute | solution.py:37
  (93 shorter events, 22.7 us)
Async XLA Ops:
  2.3 18.6 %collective-permute-start.13 = (f32[16,8192]{1,0:T(8,128)S(1)}, f32[16,8192]{1,0:T(8,128)S(1)}, u32[]{:S(2)}, u32[]{:S(2)}) collective-permute-start(f32[16,8192]{1,0:T(8,128)S(1)} %multiply_bitcast_fusion.1), channel_id=1, source_target_pairs={{0,32},{32,0},{64,96},{96,64},{128,160},{160,128},{192,224},{224,1... | collective-permute-start | bytes 1572872 | tf_op jit(solution)/shard_map/ppermute | solution.py:346
  2.4 18.6 %collective-permute-start.3 = (bf16[128,1024]{1,0:T(8,128)(2,1)}, bf16[128,1024]{1,0:T(8,128)(2,1)S(1)}, u32[]{:S(2)}, u32[]{:S(2)}) collective-permute-start(bf16[128,1024]{1,0:T(8,128)(2,1)} %bitcast.53), channel_id=1, source_target_pairs={{0,4},{1,5},{2,6},{3,7},{4,0},{5,1},{6,2},{7,3},{8,12},{9,13},{10,... | collective-permute-start | bytes 786440 | tf_op jit(solution)/shard_map/ppermute | solution.py:37
  15.8 12.2 %collective-permute-start.2 = (bf16[144,1024]{1,0:T(8,128)(2,1)S(1)}, bf16[144,1024]{1,0:T(8,128)(2,1)S(1)}, u32[]{:S(2)}, u32[]{:S(2)}) collective-permute-start(bf16[144,1024]{1,0:T(8,128)(2,1)S(1)} %pad_maximum_fusion), channel_id=1, source_target_pairs={{0,2},{1,3},{2,0},{3,1},{4,6},{5,7},{6,4},{7,5},{8,10},{9,11},{10,... | collective-permute-start | bytes 884744 | tf_op jit(solution)/shard_map/ppermute | solution.py:37
  18.9 8.5 %collective-permute-start.1 = (bf16[144,1024]{1,0:T(8,128)(2,1)S(1)}, bf16[144,1024]{1,0:T(8,128)(2,1)S(1)}, u32[]{:S(2)}, u32[]{:S(2)}) collective-permute-start(bf16[144,1024]{1,0:T(8,128)(2,1)S(1)} %pad_maximum_fusion), channel_id=1, source_target_pairs={{0,3},{1,0},{2,1},{3,2},{4,7},{5,4},{6,5},{7,6},{8,11},{9,8},{10,9... | collective-permute-start | bytes 884744 | tf_op jit(solution)/shard_map/ppermute | solution.py:37
  20.0 7.9 %collective-permute-start = (bf16[144,1024]{1,0:T(8,128)(2,1)S(1)}, bf16[144,1024]{1,0:T(8,128)(2,1)S(1)}, u32[]{:S(2)}, u32[]{:S(2)}) collective-permute-start(bf16[144,1024]{1,0:T(8,128)(2,1)S(1)} %pad_maximum_fusion), channel_id=1, source_target_pairs={{0,1},{1,2},{2,3},{3,0},{4,5},{5,6},{6,7},{7,4},{8,9},{9,10},{10,1... | collective-permute-start | bytes 884744 | tf_op jit(solution)/shard_map/ppermute | solution.py:37
  21.0 21.7 %collective-permute-start.14 = (f32[16,8192]{1,0:T(8,128)S(1)}, f32[16,8192]{1,0:T(8,128)S(1)}, u32[]{:S(2)}, u32[]{:S(2)}) collective-permute-start(f32[16,8192]{1,0:T(8,128)S(1)} %fusion.16), channel_id=1, source_target_pairs={{0,64},{32,96},{64,0},{96,32},{128,192},{160,224},{192,128},{224,1... | collective-permute-start | bytes 1572872 | tf_op jit(solution)/shard_map/ppermute | solution.py:346
  28.0 11.1 %collective-permute-start.6 = (bf16[128,1024]{1,0:T(8,128)(2,1)S(1)}, bf16[128,1024]{1,0:T(8,128)(2,1)S(1)}, u32[]{:S(2)}, u32[]{:S(2)}) collective-permute-start(bf16[128,1024]{1,0:T(8,128)(2,1)S(1)} %collective-permute-done.3.refs_2_), channel_id=1, source_target_pairs={{0,2},{1,3},{2,0},{3,1},{4,6},{5,7},{6,4},{7,5},{8,10},{9,11},{10,... | collective-permute-start | bytes 786440 | tf_op jit(solution)/shard_map/ppermute | solution.py:37
  30.3 7.8 %collective-permute-start.5 = (bf16[128,1024]{1,0:T(8,128)(2,1)S(1)}, bf16[128,1024]{1,0:T(8,128)(2,1)S(1)}, u32[]{:S(2)}, u32[]{:S(2)}) collective-permute-start(bf16[128,1024]{1,0:T(8,128)(2,1)S(1)} %collective-permute-done.3.refs_2_), channel_id=1, source_target_pairs={{0,3},{1,0},{2,1},{3,2},{4,7},{5,4},{6,5},{7,6},{8,11},{9,8},{10,9... | collective-permute-start | bytes 786440 | tf_op jit(solution)/shard_map/ppermute | solution.py:37
  31.5 7.6 %collective-permute-start.4 = (bf16[128,1024]{1,0:T(8,128)(2,1)S(1)}, bf16[128,1024]{1,0:T(8,128)(2,1)S(1)}, u32[]{:S(2)}, u32[]{:S(2)}) collective-permute-start(bf16[128,1024]{1,0:T(8,128)(2,1)S(1)} %collective-permute-done.3.refs_2_), channel_id=1, source_target_pairs={{0,1},{1,2},{2,3},{3,0},{4,5},{5,6},{6,7},{7,4},{8,9},{9,10},{10,1... | collective-permute-start | bytes 786440 | tf_op jit(solution)/shard_map/ppermute | solution.py:37
  39.3 38.6 %collective-permute-start.10 = (bf16[1024,1024]{1,0:T(8,128)(2,1)S(1)}, bf16[1024,1024]{1,0:T(8,128)(2,1)S(1)}, u32[]{:S(2)}, u32[]{:S(2)}) collective-permute-start(bf16[1024,1024]{1,0:T(8,128)(2,1)S(1)} %shard_map.111.refs_2_), channel_id=1, source_target_pairs={{0,24},{1,25},{2,26},{3,27},{4,28},{5,29},{6,30},{7,31},{8,0},{9,1... | collective-permute-start | bytes 6291464 | tf_op jit(solution)/shard_map/ppermute | solution.py:37
  40.1 37.7 %collective-permute-start.9 = (bf16[1024,1024]{1,0:T(8,128)(2,1)S(1)}, bf16[1024,1024]{1,0:T(8,128)(2,1)S(1)}, u32[]{:S(2)}, u32[]{:S(2)}) collective-permute-start(bf16[1024,1024]{1,0:T(8,128)(2,1)S(1)} %shard_map.111.refs_2_), channel_id=1, source_target_pairs={{0,8},{1,9},{2,10},{3,11},{4,12},{5,13},{6,14},{7,15},{8,16},{9,17... | collective-permute-start | bytes 6291464 | tf_op jit(solution)/shard_map/ppermute | solution.py:37
  42.7 22.5 %collective-permute-start.15 = (f32[16,8192]{1,0:T(8,128)S(1)}, f32[16,8192]{1,0:T(8,128)S(1)}, u32[]{:S(2)}, u32[]{:S(2)}) collective-permute-start(f32[16,8192]{1,0:T(8,128)S(1)} %add.81), channel_id=1, source_target_pairs={{0,128},{32,160},{64,192},{96,224},{128,0},{160,32},{192,64},{224,... | collective-permute-start | bytes 1572872 | tf_op jit(solution)/shard_map/ppermute | solution.py:346
  44.2 21.0 %copy-start.4 = (f32[16,8192]{1,0:T(8,128)S(1)}, f32[16,8192]{1,0:T(8,128)}, u32[]{:S(2)}) copy-start(f32[16,8192]{1,0:T(8,128)} %param.12) | copy-start | bytes 1572868
  44.2 21.0 %copy-start.5 = (f32[16,8192]{1,0:T(8,128)S(1)}, f32[16,8192]{1,0:T(8,128)}, u32[]{:S(2)}) copy-start(f32[16,8192]{1,0:T(8,128)} %param.13) | copy-start | bytes 1572868
  45.0 21.4 %copy-start = (bf16[512,4096]{1,0:T(8,128)(2,1)S(1)}, bf16[512,4096]{1,0:T(8,128)(2,1)}, u32[]{:S(2)}) copy-start(bf16[512,4096]{1,0:T(8,128)(2,1)} %refs_0_.5) | copy-start | bytes 12582916
  45.7 27.4 %collective-permute-start.7 = (f16[512,1024]{1,0:T(8,128)(2,1)S(1)}, f16[512,1024]{1,0:T(8,128)(2,1)S(1)}, u32[]{:S(2)}, u32[]{:S(2)}) collective-permute-start(f16[512,1024]{1,0:T(8,128)(2,1)S(1)} %multiply_convert_fusion.7), channel_id=1, source_target_pairs={{0,1},{1,2},{2,3},{3,0},{4,5},{5,6},{6,7},{7,4},{8,9},{9,10},{10,1... | collective-permute-start | bytes 3145736 | tf_op jit(solution)/shard_map/ppermute | solution.py:37
  46.3 26.9 %collective-permute-start.8 = (f16[512,1024]{1,0:T(8,128)(2,1)S(1)}, f16[512,1024]{1,0:T(8,128)(2,1)S(1)}, u32[]{:S(2)}, u32[]{:S(2)}) collective-permute-start(f16[512,1024]{1,0:T(8,128)(2,1)S(1)} %multiply_convert_fusion.6), channel_id=1, source_target_pairs={{0,3},{1,0},{2,1},{3,2},{4,7},{5,4},{6,5},{7,6},{8,11},{9,8},{10,9... | collective-permute-start | bytes 3145736 | tf_op jit(solution)/shard_map/ppermute | solution.py:37
  77.9 13.8 %collective-permute-start.18 = (f16[256,1024]{1,0:T(8,128)(2,1)S(1)}, f16[256,1024]{1,0:T(8,128)(2,1)S(1)}, u32[]{:S(2)}, u32[]{:S(2)}) collective-permute-start(f16[256,1024]{1,0:T(8,128)(2,1)S(1)} %get-tuple-element.99), channel_id=1, source_target_pairs={{0,3},{1,0},{2,1},{3,2},{4,7},{5,4},{6,5},{7,6},{8,11},{9,8},{10,9... | collective-permute-start | bytes 1572872 | tf_op jit(solution)/shard_map/ppermute | solution.py:37
  79.5 16.0 %collective-permute-start.16 = (f16[256,1024]{1,0:T(8,128)(2,1)S(1)}, f16[256,1024]{1,0:T(8,128)(2,1)S(1)}, u32[]{:S(2)}, u32[]{:S(2)}) collective-permute-start(f16[256,1024]{1,0:T(8,128)(2,1)S(1)} %get-tuple-element.95), channel_id=1, source_target_pairs={{0,1},{1,2},{2,3},{3,0},{4,5},{5,6},{6,7},{7,4},{8,9},{9,10},{10,1... | collective-permute-start | bytes 1572872 | tf_op jit(solution)/shard_map/ppermute | solution.py:37
  80.8 21.3 %collective-permute-start.12 = (bf16[512,1024]{1,0:T(8,128)(2,1)S(1)}, bf16[512,1024]{1,0:T(8,128)(2,1)S(1)}, u32[]{:S(2)}, u32[]{:S(2)}) collective-permute-start(bf16[512,1024]{1,0:T(8,128)(2,1)S(1)} %slice.173), channel_id=1, source_target_pairs={{0,24},{1,25},{2,26},{3,27},{4,28},{5,29},{6,30},{7,31},{8,0},{9,1... | collective-permute-start | bytes 3145736 | tf_op jit(solution)/shard_map/ppermute | solution.py:37
  80.9 21.2 %collective-permute-start.11 = (bf16[512,1024]{1,0:T(8,128)(2,1)S(1)}, bf16[512,1024]{1,0:T(8,128)(2,1)S(1)}, u32[]{:S(2)}, u32[]{:S(2)}) collective-permute-start(bf16[512,1024]{1,0:T(8,128)(2,1)S(1)} %slice.172), channel_id=1, source_target_pairs={{0,8},{1,9},{2,10},{3,11},{4,12},{5,13},{6,14},{7,15},{8,16},{9,17... | collective-permute-start | bytes 3145736 | tf_op jit(solution)/shard_map/ppermute | solution.py:37
  96.5 19.4 %collective-permute-start.20 = (f16[144,1024]{1,0:T(8,128)(2,1)S(1)}, f16[144,1024]{1,0:T(8,128)(2,1)S(1)}, u32[]{:S(2)}, u32[]{:S(2)}) collective-permute-start(f16[144,1024]{1,0:T(8,128)(2,1)S(1)} %concatenate.25), channel_id=1, source_target_pairs={{0,8},{1,9},{2,10},{3,11},{4,12},{5,13},{6,14},{7,15},{8,16},{9,17... | collective-permute-start | bytes 884744 | tf_op jit(solution)/shard_map/ppermute | solution.py:37
  100.0 16.0 %collective-permute-start.22 = (f16[144,1024]{1,0:T(8,128)(2,1)S(1)}, f16[144,1024]{1,0:T(8,128)(2,1)S(1)}, u32[]{:S(2)}, u32[]{:S(2)}) collective-permute-start(f16[144,1024]{1,0:T(8,128)(2,1)S(1)} %slice_select_fusion.1), channel_id=1, source_target_pairs={{0,16},{1,17},{2,18},{3,19},{4,20},{5,21},{6,22},{7,23},{8,24},{9,... | collective-permute-start | bytes 884744 | tf_op jit(solution)/shard_map/ppermute | solution.py:37
  100.1 15.8 %collective-permute-start.21 = (f16[144,1024]{1,0:T(8,128)(2,1)S(1)}, f16[144,1024]{1,0:T(8,128)(2,1)S(1)}, u32[]{:S(2)}, u32[]{:S(2)}) collective-permute-start(f16[144,1024]{1,0:T(8,128)(2,1)S(1)} %concatenate.26), channel_id=1, source_target_pairs={{0,24},{1,25},{2,26},{3,27},{4,28},{5,29},{6,30},{7,31},{8,0},{9,1... | collective-permute-start | bytes 884744 | tf_op jit(solution)/shard_map/ppermute | solution.py:37
  102.1 21.5 %collective-permute-start.17 = (f16[512,1024]{1,0:T(8,128)(2,1)S(1)}, f16[512,1024]{1,0:T(8,128)(2,1)S(1)}, u32[]{:S(2)}, u32[]{:S(2)}) collective-permute-start(f16[512,1024]{1,0:T(8,128)(2,1)S(1)} %multiply_convert_fusion.4), channel_id=1, source_target_pairs={{0,1},{1,2},{2,3},{3,0},{4,5},{5,6},{6,7},{7,4},{8,9},{9,10},{10,1... | collective-permute-start | bytes 3145736 | tf_op jit(solution)/shard_map/ppermute | solution.py:37
  102.2 25.4 %collective-permute-start.19 = (f16[512,1024]{1,0:T(8,128)(2,1)S(1)}, f16[512,1024]{1,0:T(8,128)(2,1)S(1)}, u32[]{:S(2)}, u32[]{:S(2)}) collective-permute-start(f16[512,1024]{1,0:T(8,128)(2,1)S(1)} %multiply_convert_fusion.3), channel_id=1, source_target_pairs={{0,3},{1,0},{2,1},{3,2},{4,7},{5,4},{6,5},{7,6},{8,11},{9,8},{10,9... | collective-permute-start | bytes 3145736 | tf_op jit(solution)/shard_map/ppermute | solution.py:37
  128.1 11.5 %collective-permute-start.24 = (f16[256,1024]{1,0:T(8,128)(2,1)S(1)}, f16[256,1024]{1,0:T(8,128)(2,1)S(1)}, u32[]{:S(2)}, u32[]{:S(2)}) collective-permute-start(f16[256,1024]{1,0:T(8,128)(2,1)S(1)} %get-tuple-element.118), channel_id=1, source_target_pairs={{0,3},{1,0},{2,1},{3,2},{4,7},{5,4},{6,5},{7,6},{8,11},{9,8},{10,9... | collective-permute-start | bytes 1572872 | tf_op jit(solution)/shard_map/ppermute | solution.py:37
  131.8 10.7 %collective-permute-start.23 = (f16[256,1024]{1,0:T(8,128)(2,1)S(1)}, f16[256,1024]{1,0:T(8,128)(2,1)S(1)}, u32[]{:S(2)}, u32[]{:S(2)}) collective-permute-start(f16[256,1024]{1,0:T(8,128)(2,1)S(1)} %get-tuple-element.117), channel_id=1, source_target_pairs={{0,1},{1,2},{2,3},{3,0},{4,5},{5,6},{6,7},{7,4},{8,9},{9,10},{10,1... | collective-permute-start | bytes 1572872 | tf_op jit(solution)/shard_map/ppermute | solution.py:37
  132.6 21.7 %collective-permute-start.28 = (f16[144,1024]{1,0:T(8,128)(2,1)S(1)}, f16[144,1024]{1,0:T(8,128)(2,1)S(1)}, u32[]{:S(2)}, u32[]{:S(2)}) collective-permute-start(f16[144,1024]{1,0:T(8,128)(2,1)S(1)} %pad_maximum_fusion.1), channel_id=1, source_target_pairs={{0,4},{1,5},{2,6},{3,7},{4,0},{5,1},{6,2},{7,3},{8,12},{9,13},{10,... | collective-permute-start | bytes 884744 | tf_op jit(solution)/shard_map/ppermute | solution.py:37
  143.5 13.1 %collective-permute-start.25 = (f16[144,1024]{1,0:T(8,128)(2,1)S(1)}, f16[144,1024]{1,0:T(8,128)(2,1)S(1)}, u32[]{:S(2)}, u32[]{:S(2)}) collective-permute-start(f16[144,1024]{1,0:T(8,128)(2,1)S(1)} %concatenate.29), channel_id=1, source_target_pairs={{0,8},{1,9},{2,10},{3,11},{4,12},{5,13},{6,14},{7,15},{8,16},{9,17... | collective-permute-start | bytes 884744 | tf_op jit(solution)/shard_map/ppermute | solution.py:37
  145.7 10.9 %collective-permute-start.26 = (f16[144,1024]{1,0:T(8,128)(2,1)S(1)}, f16[144,1024]{1,0:T(8,128)(2,1)S(1)}, u32[]{:S(2)}, u32[]{:S(2)}) collective-permute-start(f16[144,1024]{1,0:T(8,128)(2,1)S(1)} %concatenate.30), channel_id=1, source_target_pairs={{0,24},{1,25},{2,26},{3,27},{4,28},{5,29},{6,30},{7,31},{8,0},{9,1... | collective-permute-start | bytes 884744 | tf_op jit(solution)/shard_map/ppermute | solution.py:37
  152.1 9.9 %collective-permute-start.27 = (f16[144,1024]{1,0:T(8,128)(2,1)S(1)}, f16[144,1024]{1,0:T(8,128)(2,1)S(1)}, u32[]{:S(2)}, u32[]{:S(2)}) collective-permute-start(f16[144,1024]{1,0:T(8,128)(2,1)S(1)} %slice_select_fusion), channel_id=1, source_target_pairs={{0,16},{1,17},{2,18},{3,19},{4,20},{5,21},{6,22},{7,23},{8,24},{9,... | collective-permute-start | bytes 884744 | tf_op jit(solution)/shard_map/ppermute | solution.py:37
  (5 other events, 55.2 us)
